TPU v7x, 32 devices: a whole 2x2x4 slice. The times are simulated.
32 devices in a mesh: lo: 8 (over z, y), hi: 4 (over x, core).
Axes of the slice: x: 2, y: 2, z: 4, core: 2. Of those that a mesh axis runs over, the one named last changes fastest.
Arguments:
- contribution: float32 [4, 8, 1024, 1024], P('hi', 'lo'), as said below
- pivot_one: float32 [4, 8, 384, 768], P('hi', 'lo'), as said below
- rows_one: float32 [4, 8, 768, 2304], P('hi', 'lo'), as said below
- pivot_two: float32 [4, 8, 192, 768], P('hi', 'lo'), as said below
- rows_two: float32 [4, 8, 384, 2304], P('hi', 'lo'), as said below
- map_one: int32 [4, 8, 8], replicated, may hold values from 0 to 17, as said below
- map_two: int32 [4, 4, 12], replicated, may hold values from 0 to 17, as said below
- fill_one: int32 [4, 4, 12, 6], replicated, may hold values 0 or 1
- fill_two: int32 [2, 4, 12, 6], replicated, may hold values 0 or 1
- live_one: int32 [4, 4], replicated, may hold values from 3 to 6, as said below
- live_two: int32 [2, 4], replicated, may hold values from 3 to 6, as said below
Outputs:
- lower_one: float32 [4, 8, 384, 768], P('hi', 'lo')
- panel_one: float32 [4, 8, 768, 768], P('hi', 'lo')
- lower_two: float32 [4, 8, 192, 768], P('hi', 'lo')
- panel_two: float32 [4, 8, 384, 768], P('hi', 'lo')
- schur_two: float32 [4, 8, 384, 1536], P('hi', 'lo')
Inputs may be any that keep to these rules, and one draw needn't show every extreme that they name: `contribution`: symmetric and negative semidefinite: minus a Gram matrix, divided by 1024. `pivot_one`: with rows_one, the rows of a symmetric matrix of each front with a dominant diagonal. `rows_one`: with pivot_one, the rows of a symmetric matrix of each front with a dominant diagonal. `pivot_two`: with rows_two, the rows of a symmetric matrix of each front with a dominant diagonal. `rows_two`: with pivot_two, the rows of a symmetric matrix of each front with a dominant diagonal. `map_one`: each device's list names 8 distinct tiles. `map_two`: each front's list names 12 distinct tiles. `live_one`: both ends reached in every draw. `live_two`: both ends reached in every draw.
All inputs are finite; a program needn't handle non-finite values.
Results may differ from a plain program's by a relative error of at most 0.0003.
Values sent between devices are 32-bit elements; how exact they have to be, the bound alone decides.
No kernel may reach another device: no remote copies, remote signals or barrier semaphores. Data moves between devices by JAX's collectives and lax.ppermute only.
A program may use at most 192 MiB of HBM per device.

v0:
```python
import functools

import jax
import jax.numpy as jnp
import numpy as np
from jax import lax
from jax.experimental import pallas as pl
from jax.experimental.pallas import tpu as pltpu
from jax.sharding import PartitionSpec as P

TILE = 128
HALF = TILE // 2
CT = 8
P1T = 6
U1T = 12
P2T = 6
U2T = 12
ROWS = 8

HALF_U = U1T // 2
QUARTER = U2T // 4
PIVOT = P1T * TILE
SECOND = P2T * TILE

TRI_C = [(a, b) for a in range(CT) for b in range(a + 1)]
TRI_U = [(a, b) for a in range(HALF_U) for b in range(a + 1)]
TRI_P = [(a, b) for a in range(P1T // 2) for b in range(a + 1)]
BELOW_C = [(a, b) for a, b in TRI_C if a != b]
BELOW_U = [(a, b) for a, b in TRI_U if a != b]
BELOW_P = [(a, b) for a, b in TRI_P if a != b]
DIAG_FIRST = CT + P1T // 2
N_FIRST = len(BELOW_C) + len(BELOW_P) + (DIAG_FIRST + 1) // 2
N_OWN = len(BELOW_U) + (HALF_U + 1) // 2
UNITS = SECOND // HALF
OWN_UNITS = UNITS // 4
REACH = UNITS // 2 + 1
N_UNIT = OWN_UNITS * REACH
N_WIDE = (N_UNIT + 1) // 2
N_TWO = QUARTER * P2T
N_MAIN = 30
N_TWO_A = 5
N_TWO_B = 11
N_OFF = (P1T // 2) ** 2
N_PIV = P1T * P1T
N_COUP = HALF_U * P1T
N_TRI = len(TRI_U)
N_CROSS = HALF_U * HALF_U
N_CROSS_A = N_CROSS // 2
N_OVER = N_COUP - N_MAIN + N_TWO - N_TWO_A - N_TWO_B
S_COUP = N_PIV
S_OWN = S_COUP + N_COUP
S_FAR = S_OWN + N_TRI
S_CROSS = S_FAR + N_COUP
S_OTH = S_CROSS + N_CROSS
N_FRONT = S_OTH + N_TRI
G_COUP = P2T * P2T
G_TRAIL = G_COUP + U2T * P2T
G_NONE = G_TRAIL + QUARTER * U2T

NT = (((1,), (1,)), ((), ()))
NN = (((1,), (0,)), ((), ()))
F32 = jnp.float32


def split(x):
    high = x.astype(jnp.bfloat16)
    return high, (x - high.astype(F32)).astype(jnp.bfloat16)


def dot3(a, b, dims):
    def one(p, q):
        return lax.dot_general(p, q, dims, preferred_element_type=F32)

    return one(a[0], b[0]) + (one(a[0], b[1]) + one(a[1], b[0]))


def times_inverse(block, parts):
    wide = 2 * TILE
    size = parts[0].shape[0]
    block = split(block)
    return jnp.concatenate(
        [
            dot3([p[:, : c + wide] for p in block], [q[c : c + wide, : c + wide] for q in parts], NT)
            for c in range(0, size, wide)
        ],
        axis=1,
    )


def mul(a, b, dims):
    return dot3(split(a), split(b), dims)


def factor_half(block, width):
    groups = HALF // ROWS
    sub = lax.broadcasted_iota(jnp.int32, (ROWS, TILE), 0)
    lane = lax.broadcasted_iota(jnp.int32, (ROWS, TILE), 1)

    def full(x):
        return jnp.broadcast_to(x, (ROWS, TILE))

    wide = jnp.concatenate([block, jnp.zeros((HALF, HALF), F32)], axis=1)
    a = [
        jnp.where(lane == sub + ROWS * g + HALF, 1.0, wide[ROWS * g : ROWS * g + ROWS])
        for g in range(groups)
    ]
    rows = [None] * HALF
    for j in range(0, HALF, width):
        gj, o = j // ROWS, j % ROWS
        cols = {g: [full(a[g][:, j + i : j + i + 1]) for i in range(width)] for g in range(gj, groups)}
        s = [
            [full(cols[gj][k][o + i : o + i + 1, :]) if k <= i else None for k in range(width)]
            for i in range(width)
        ]
        u = [full(a[gj][o + i : o + i + 1, :]) for i in range(width)]
        inv = [None] * width
        low = [[None] * width for _ in range(width)]
        for k in range(width):
            inv[k] = lax.rsqrt(s[k][k])
            for i in range(k + 1, width):
                low[i][k] = s[i][k] * inv[k]
            for i in range(k + 1, width):
                for q in range(k + 1, i + 1):
                    s[i][q] = s[i][q] - low[i][k] * low[q][k]
        for i in range(width):
            for k in range(i):
                u[i] = u[i] - low[i][k] * u[k]
            u[i] = u[i] * inv[i]
            rows[j + i] = u[i]
        for g in range(gj if o + width < ROWS else gj + 1, groups):
            c = cols[g]
            for i in range(width):
                for k in range(i):
                    c[i] = c[i] - c[k] * low[i][k]
                c[i] = c[i] * inv[i]
            for i in range(width):
                a[g] = a[g] - c[i] * u[i]
    out = []
    for g in range(groups):
        v = rows[ROWS * g]
        for i in range(1, ROWS):
            v = jnp.where(sub == i, rows[ROWS * g + i], v)
        out.append(v)
    both = jnp.concatenate(out, axis=0)
    return both[:, :HALF], both[:, HALF:]


def factor(a, low, inv, tiles, width, start=0, stop=None):
    stop = tiles if stop is None else stop
    d = a[start * TILE : (start + 1) * TILE, start * TILE : (start + 1) * TILE]
    zero = jnp.zeros((HALF, HALF), F32)
    ri = lax.broadcasted_iota(jnp.int32, (HALF, HALF), 0)
    ci = lax.broadcasted_iota(jnp.int32, (HALF, HALF), 1)
    for k in range(start, stop):
        k0, k1, k2 = k * TILE, (k + 1) * TILE, (k + 2) * TILE
        u1, w1 = factor_half(d[:HALF, :HALF], width)
        l21 = mul(d[HALF:, :HALF], w1, NT)
        u2, w2 = factor_half(d[HALF:, HALF:] - mul(l21, l21, NT), width)
        w21 = -mul(w2, mul(l21, w1, NN), NN)
        w = jnp.concatenate([jnp.concatenate([w1, zero], 1), jnp.concatenate([w21, w2], 1)], 0)
        ws = split(w)
        inv[k0:k1, k0:k1] = w
        if k + 1 < tiles:
            p = dot3(split(a[k1:k2, k0:k1]), ws, NT)
            low[k1:k2, k0:k1] = p
            ps = split(p)
            d = a[k1:k2, k1:k2] - dot3(ps, ps, NT)
        l1 = jnp.where(ri >= ci, u1.T, 0.0)
        l2 = jnp.where(ri >= ci, u2.T, 0.0)
        low[k0:k1, k0:k1] = jnp.concatenate(
            [jnp.concatenate([l1, zero], 1), jnp.concatenate([l21, l2], 1)], 0
        )
        if k + 2 < tiles:
            low[k2:, k0:k1] = dot3(split(a[k2:, k0:k1]), ws, NT)
            for j in range(k + 1, tiles):
                j0 = j * TILE
                top = max(j0, k2)
                a[top:, j0 : j0 + TILE] = a[top:, j0 : j0 + TILE] - mul(
                    low[top:, k0:k1], low[j0 : j0 + TILE, k0:k1], NT
                )
        if k > 0:
            x = mul(low[k0:k1, 0:k0], inv[0:k0, 0:k0], NN)
            inv[k0:k1, 0:k0] = -dot3(ws, split(x), NN)
        if k + 1 < tiles:
            rest = jnp.zeros((TILE, (tiles - k - 1) * TILE), F32)
            low[k0:k1, k1:] = rest
            inv[k0:k1, k1:] = rest
    if stop < tiles:
        a[k1:k2, k1:k2] = d


def padded(a, tile_of, live, tiles):
    ri = lax.broadcasted_iota(jnp.int32, (TILE, TILE), 0)
    ci = lax.broadcasted_iota(jnp.int32, (TILE, TILE), 1)
    eye = jnp.where(ri == ci, 1.0, 0.0)
    for i in range(tiles):
        kept = (jnp.int32(i) < live).astype(F32)
        for j in range(i + 1):
            value = tile_of(i, j) * kept
            if i == j:
                value = value + eye * (1.0 - kept)
            a[i * TILE : (i + 1) * TILE, j * TILE : (j + 1) * TILE] = value


def copy_all(pairs, sems):
    copies = [pltpu.make_async_copy(src, dst, sems.at[n]) for n, (src, dst) in enumerate(pairs)]
    for c in copies:
        c.start()
    for c in copies:
        c.wait()


def tile_at(ref, row, col):
    return ref.at[
        pl.ds(pl.multiple_of(row * TILE, TILE), TILE), pl.ds(pl.multiple_of(col * TILE, TILE), TILE)
    ]


def square_index():
    return (
        lax.broadcasted_iota(jnp.int32, (TILE, TILE), 0),
        lax.broadcasted_iota(jnp.int32, (TILE, TILE), 1),
    )


def put_pairs(tiles_in, out, first):
    r, c = square_index()
    diagonals = []
    for n in range(0, len(tiles_in), 2):
        mixed = tiles_in[n]
        if n + 1 < len(tiles_in):
            mixed = jnp.where(r >= c, mixed, tiles_in[n + 1])
            diagonals.append(jnp.sum(jnp.where(r == c, tiles_in[n + 1], 0.0), axis=0, keepdims=True))
        out[pl.ds((first + n // 2) * TILE, TILE), :] = mixed
    diagonals += [jnp.zeros((1, TILE), F32)] * (ROWS - len(diagonals))
    out[pl.ds((first + (len(tiles_in) + 1) // 2) * TILE, ROWS), :] = jnp.concatenate(diagonals, axis=0)


def get_pairs(ref, first, count):
    r, c = square_index()
    base = (first + (count + 1) // 2) * TILE
    out = []
    for n in range(0, count, 2):
        mixed = ref[(first + n // 2) * TILE : (first + n // 2 + 1) * TILE, :]
        if n + 1 == count:
            out.append(mixed)
            continue
        other = mixed.T
        out.append(jnp.where(r >= c, mixed, other))
        diagonal = ref[base + n // 2 : base + n // 2 + 1, :]
        out.append(jnp.where(r == c, diagonal, jnp.where(r < c, mixed, other)))
    return out


def message_tile(ref, n):
    return ref[pl.ds(pl.multiple_of(n * TILE, TILE), TILE), :]


def pack_first(tab, block, pivot, out, square, sems):
    side = tab[CT]
    pairs = []
    for n, (a, b) in enumerate(BELOW_C):
        pairs.append((tile_at(block, tab[a], tab[b]), out.at[pl.ds(n * TILE, TILE)]))
    first = len(BELOW_C)
    for n, (a, b) in enumerate(BELOW_P):
        pairs.append(
            (tile_at(pivot, a, side * (P1T // 2) + b), out.at[pl.ds((first + n) * TILE, TILE)])
        )
    for a in range(CT):
        pairs.append((tile_at(block, tab[a], tab[a]), square.at[a]))
    for a in range(P1T // 2):
        pairs.append((tile_at(pivot, a, side * (P1T // 2) + a), square.at[CT + a]))
    copy_all(pairs, sems)
    put_pairs([square[n] for n in range(DIAG_FIRST)], out, first + len(BELOW_P))


def pack_rest(
    tab, block, pivot, rows, pivot_second, second,
    coup, own, kept, cross, off, coup_two, units, units_sent, main, two_sent_a, two_sent_b, over,
    strips, sems,
):
    side = tab[CT]
    order = CT + 1
    local = order + CT
    quarter = tab[local + U1T]
    pairs = []
    for r in range(HALF_U):
        row = tab[local + r] - side * HALF_U
        for c in range(P1T):
            pairs.append((tile_at(rows, row, c), coup.at[r * P1T + c]))
    for n, (a, b) in enumerate(TRI_U):
        row = tab[local + a] - side * HALF_U
        pairs.append((tile_at(rows, row, P1T + tab[local + b]), own.at[n]))
    for n, (a, b) in enumerate(TRI_C):
        pairs.append((tile_at(block, tab[order + a], tab[order + b]), kept.at[n]))
    for i in range(HALF_U):
        row = tab[local + i] - side * HALF_U
        for k in range(HALF_U):
            pairs.append(
                (tile_at(rows, row, P1T + tab[local + HALF_U + k]), cross.at[i * HALF_U + k])
            )
    for i in range(P1T // 2):
        for k in range(P1T // 2):
            pairs.append(
                (tile_at(pivot, i, (1 - side) * (P1T // 2) + k), off.at[i * (P1T // 2) + k])
            )
    for n, (i, k) in enumerate(TRI_P):
        pairs.append((tile_at(pivot, i, side * (P1T // 2) + k), off.at[N_OFF + n]))
    for r in range(QUARTER):
        for c in range(P2T):
            pairs.append((tile_at(second, r, c), coup_two.at[r * P2T + c]))
    first = local + U1T + 1
    for p in range(N_COUP):
        n = tab[first + p]
        row = tab[local + n // P1T] - side * HALF_U
        sent = main.at[p] if p < N_MAIN else over.at[p - N_MAIN]
        pairs.append((tile_at(rows, row, n % P1T), sent))
    first += N_COUP
    for p in range(N_TWO):
        n = tab[first + p]
        if p < N_TWO_A:
            sent = two_sent_a.at[p]
        elif p < N_TWO_A + N_TWO_B:
            sent = two_sent_b.at[p - N_TWO_A]
        else:
            sent = over.at[p + N_COUP - N_MAIN - N_TWO_A - N_TWO_B]
        pairs.append((tile_at(second, n // P2T, n % P2T), sent))
    far = []
    for i in range(OWN_UNITS):
        for d in range(REACH):
            col = (quarter * OWN_UNITS + i - d + UNITS) % UNITS
            far.append(col % 2)
            source = pivot_second.at[
                pl.ds(i * HALF, HALF), pl.ds(pl.multiple_of(col // 2 * TILE, TILE), TILE)
            ]
            pairs.append((source, strips.at[i * REACH + d]))
    copy_all(pairs, sems)
    lane = lax.broadcasted_iota(jnp.int32, (HALF, TILE), 1)

    def placed(n, half):
        strip = strips[n]
        return jnp.where(far[n] == half, strip, pltpu.roll(strip, HALF, 1))

    for n in range(N_WIDE):
        strip = placed(2 * n, 0)
        if 2 * n + 1 < N_UNIT:
            strip = jnp.where(lane < HALF, strip, placed(2 * n + 1, 1))
        units[n * HALF : (n + 1) * HALF, :] = strip
        units_sent[n * HALF : (n + 1) * HALF, :] = strip


def after(array, *others):
    def kernel(*refs):
        pass

    return pl.pallas_call(
        kernel,
        out_shape=jax.ShapeDtypeStruct(array.shape, array.dtype),
        in_specs=[HBM] * (1 + len(others)),
        out_specs=HBM,
        input_output_aliases={0: 0},
        name="after",
        cost_estimate=CHEAP,
    )(array, *others)


def part_of(array):
    return array[(0,) * (array.ndim - 2)][:ROWS]


T_SIDE = 0
T_LIVE = 1
T_LOCAL = 2
T_FILL = T_LOCAL + U1T
T_SLOT = T_FILL + U1T * P1T
T_SLOT_FAR = T_SLOT + CT * CT
T_PLACE = T_SLOT_FAR + CT * CT


def panel_rows(tile_of, count, live, parts, put):
    for r in range(0, count, 2):
        block = jnp.concatenate(
            [
                jnp.concatenate([tile_of(r + i, c) for c in range(P1T)], axis=1)
                for i in range(2)
            ],
            axis=0,
        )
        lane = lax.broadcasted_iota(jnp.int32, block.shape, 1)
        block = jnp.where(lane < live * TILE, block, 0.0)
        put(r, times_inverse(block, parts))


def first_kernel(
    tab, mine, theirs, coup, own, cross, off,
    lower_out, inv_high, inv_low, panel_high, panel_low, rows_out, own_out, own_sent, far_out,
    front, a, low, inv, sem,
):
    side = tab[T_SIDE]
    live = tab[T_LIVE]
    half = P1T // 2
    square = get_pairs(theirs, len(BELOW_C) + len(BELOW_P), DIAG_FIRST)
    front[0:N_PIV] = jnp.zeros((N_PIV, TILE, TILE), F32)
    for n, (i, k) in enumerate(TRI_P):
        front[(side * half + i) * P1T + side * half + k] = off[N_OFF + n]
        if i == k:
            tile = square[CT + i]
        else:
            tile = message_tile(theirs, len(BELOW_C) + BELOW_P.index((i, k)))
        front[((1 - side) * half + i) * P1T + (1 - side) * half + k] = tile
    for i in range(half):
        for k in range(half):

            @pl.when(side == 0)
            def _():
                front[(half + k) * P1T + i] = off[i * half + k].T

            @pl.when(side != 0)
            def _():
                front[(half + i) * P1T + k] = off[i * half + k]

    def scale(n, carry):
        front[S_COUP + n] = coup[n] * tab[T_FILL + n].astype(F32)
        front[S_FAR + n] = jnp.zeros((TILE, TILE), F32)
        front[S_CROSS + n] = cross[n]
        return carry

    lax.fori_loop(0, N_COUP, scale, 0)

    def copy(n, carry):
        front[S_OWN + n] = own[n]
        front[S_OTH + n] = jnp.zeros((TILE, TILE), F32)
        return carry

    lax.fori_loop(0, N_TRI, copy, 0)
    for i in range(CT):

        def extend(k, carry, i=i):
            here = tab[T_SLOT + i * CT + k]
            front[here] = front[here] + mine[tri(i, 0) + k]
            return carry

        lax.fori_loop(0, i + 1, extend, 0)

        def extend_far(k, carry, i=i):
            there = tab[T_SLOT_FAR + i * CT + k]
            front[there] = front[there] + message_tile(theirs, i * (i - 1) // 2 + k)
            return carry

        lax.fori_loop(0, i, extend_far, 0)
        there = tab[T_SLOT_FAR + i * CT + i]
        front[there] = front[there] + square[i]
    leave = pltpu.make_async_copy(front.at[pl.ds(S_FAR, S_OTH - S_FAR)], far_out, sem)
    leave.start()
    padded(a, lambda i, j: front[i * P1T + j], live, P1T)
    factor(a, low, inv, P1T, 4)
    inv_high[...], inv_low[...] = split(inv[...])
    lower_out[...] = low[pl.ds(pl.multiple_of(side * (PIVOT // 2), TILE), PIVOT // 2), :]

    def put(r, rows):
        wide = slice(r * TILE, (r + 2) * TILE)
        panel_high[wide, :], panel_low[wide, :] = split(rows)
        for i in range(2):
            place = tab[T_LOCAL + r + i] - side * HALF_U
            rows_out[pl.ds(pl.multiple_of(place * TILE, TILE), TILE), :] = rows[
                i * TILE : (i + 1) * TILE
            ]

    panel_rows(lambda r, c: front[S_COUP + r * P1T + c], HALF_U, live, (inv_high[...], inv_low[...]), put)
    for i in range(HALF_U):
        left = [p[i * TILE : (i + 1) * TILE, :] for p in (panel_high, panel_low)]
        right = [p[0 : (i + 1) * TILE, :] for p in (panel_high, panel_low)]
        product = dot3(left, right, NT)
        for k in range(i + 1):
            n = S_OWN + tri(i, k)
            front[n] = front[n] - product[:, k * TILE : (k + 1) * TILE]
    put_own([front[S_OWN + n] for n in range(N_TRI)], own_out)
    put_own([front[S_OWN + n] for n in range(N_TRI)], own_sent)
    leave.wait()


def choose(at, parts):
    value = None
    base = sum(count for _, _, count in parts)
    for ref, first, count in reversed(parts):
        base -= count
        tile = ref[first + jnp.clip(at - base, 0, count - 1)]
        value = tile if value is None else jnp.where(at < base + count, tile, value)
    return value


def second_kernel(
    which, tab, far, main, over, inv_high, inv_low, panel_high, panel_low, cross,
    rows_far, cross_far, sems,
):
    wide = HALF_U // 2
    copies = [(far.at[pl.ds(which * wide * P1T, wide * P1T)], rows_far)]
    for i in range(HALF_U):
        copies.append(
            (
                far.at[pl.ds(N_COUP + i * HALF_U + which * wide, wide)],
                cross_far.at[pl.ds(i * wide, wide)],
            )
        )
    copies = [pltpu.make_async_copy(src, dst, sems.at[n]) for n, (src, dst) in enumerate(copies)]
    for c in copies:
        c.start()
    live = tab[T_LIVE]
    parts = inv_high[...], inv_low[...]

    def tile_of(r, c):
        n = (which * wide + r) * P1T + c
        tile = choose(tab[T_PLACE + n], [(main, 0, N_MAIN), (over, 0, N_COUP - N_MAIN)])
        return rows_far[r * P1T + c] + tile * tab[T_FILL + N_COUP + n].astype(F32)

    for c in copies:
        c.wait()
    block = jnp.concatenate(
        [jnp.concatenate([tile_of(r, c) for c in range(P1T)], axis=1) for r in range(wide)], axis=0
    )
    lane = lax.broadcasted_iota(jnp.int32, block.shape, 1)
    block = jnp.where(lane < live * TILE, block, 0.0)
    right = split(times_inverse(block, parts))
    for i in range(0, HALF_U, 2):
        left = [p[i * TILE : (i + 2) * TILE, :] for p in (panel_high, panel_low)]
        product = dot3(left, right, NT)
        for q in range(2):
            for k in range(wide):
                n = (i + q) * wide + k
                cross[n] = (
                    cross_far[n] - product[q * TILE : (q + 1) * TILE, k * TILE : (k + 1) * TILE]
                )


def put_own(block, out):
    for n, (a, b) in enumerate(BELOW_U):
        out[n * TILE : (n + 1) * TILE, :] = block[tri(a, b)]
    put_pairs([block[tri(a, a)] for a in range(HALF_U)], out, len(BELOW_U))


def get_own(ref, out):
    for n, (i, k) in enumerate(BELOW_U):
        out[tri(i, k)] = message_tile(ref, n)
    for i, tile in enumerate(get_pairs(ref, len(BELOW_U), HALF_U)):
        out[tri(i, i)] = tile


Q_LIVE = 0
Q_MINE = 1
Q_FILL = 5
Q_DIRECT = Q_FILL + U2T * P2T
Q_TURNED = Q_DIRECT + 2 * U1T * U1T
Q_PLACE = Q_TURNED + 2 * U1T * U1T


def extend_cross(tab, ref, g, front, which):
    wide = HALF_U // 2
    extend_two(tab, ref, g, front, 0, HALF_U + which * wide, False, 0, G_NONE, wide)


def extend_two(tab, ref, g, front, rows, cols, triangle, low, high, wide=HALF_U):
    for i in range(HALF_U):

        def one(k, carry, i=i):
            at = front * U1T * U1T + (rows + i) * U1T + cols + k
            n = (tri(i, 0) if triangle else i * wide) + k
            direct = tab[Q_DIRECT + at]
            turned = tab[Q_TURNED + at]

            @pl.when((direct >= low) & (direct < high))
            def _():
                g[direct - low] = g[direct - low] + ref[n]

            @pl.when((turned >= low) & (turned < high))
            def _():
                g[turned - low] = g[turned - low] + ref[n].T

            return carry

        lax.fori_loop(0, i + 1 if triangle else wide, one, 0)


def add_units(tab, g, units, s):
    lane = lax.broadcasted_iota(jnp.int32, (HALF, TILE), 1)
    for i in range(OWN_UNITS):
        row = tab[Q_MINE + s] * OWN_UNITS + i
        for d in range(REACH):
            n = i * REACH + d
            col = (row - d + UNITS) % UNITS
            strip = units[n // 2 * HALF : (n // 2 + 1) * HALF, :]
            here = n % 2

            def add(r, c, block):
                slot = r // 2 * P2T + c // 2
                start = pl.multiple_of(r % 2 * HALF, HALF)
                old = g[slot, pl.ds(start, HALF), :]
                g[slot, pl.ds(start, HALF), :] = old + jnp.where(lane // HALF == c % 2, block, 0.0)

            @pl.when((col <= row) & ((d < REACH - 1) | (row >= UNITS // 2)))
            def _():
                add(row, col, jnp.where(col % 2 == here, strip, pltpu.roll(strip, HALF, 1)))

            if d < REACH - 1 and d > 0:

                @pl.when(col > row)
                def _():
                    turned = strip.T[here * HALF : (here + 1) * HALF, :]
                    add(col, row, jnp.concatenate([turned, turned], axis=1))


def third_kernel(tab, own0, units0, units2, second, g, block):
    def clear(n, carry):
        g[n] = jnp.zeros((TILE, TILE), F32)
        return carry

    lax.fori_loop(0, G_TRAIL, clear, 0)
    for r in range(QUARTER):
        for c in range(U2T):
            g[G_TRAIL + r * U2T + c] = second[
                r * TILE : (r + 1) * TILE, SECOND + c * TILE : SECOND + (c + 1) * TILE
            ]
    add_units(tab, g, units0, 0)
    add_units(tab, g, units2, 2)
    get_own(own0, block)
    extend_two(tab, block, g, 0, 0, 0, True, 0, G_NONE)


def more_kernel(
    tab, part, own1, cross0_a, cross0_b, cross1_a, cross1_b, oth0, units1, g, block, sem
):
    enter = pltpu.make_async_copy(part, g, sem)
    enter.start()
    get_own(oth0, block)
    enter.wait()
    add_units(tab, g, units1, 1)
    extend_cross(tab, cross0_a, g, 0, 0)
    extend_cross(tab, cross0_b, g, 0, 1)
    extend_cross(tab, cross1_a, g, 1, 0)
    extend_cross(tab, cross1_b, g, 1, 1)
    extend_two(tab, block, g, 0, HALF_U, HALF_U, True, 0, G_NONE)
    get_own(own1, block)
    extend_two(tab, block, g, 1, 0, 0, True, 0, G_NONE)


def pivot_kernel(tab, part, oth1, units3, lower_out, high_out, rest_out, g, other, a, low, inv, sem):
    enter = pltpu.make_async_copy(part.at[pl.ds(0, G_COUP)], g, sem)
    enter.start()
    get_own(oth1, other)
    enter.wait()
    add_units(tab, g, units3, 3)
    extend_two(tab, other, g, 1, HALF_U, HALF_U, True, 0, G_COUP)
    padded(a, lambda i, j: g[i * P2T + j], tab[Q_LIVE], P2T)
    factor(a, low, inv, P2T, 8)
    start = tab[Q_MINE] * (SECOND // 4)
    lower_out[...] = low[pl.ds(pl.multiple_of(start, HALF), SECOND // 4), :]
    high_out[...], rest_out[...] = split(inv[...])


def quarter_rows_of(tab, g, quarter):
    return jnp.concatenate(
        [
            jnp.concatenate([g[(quarter * QUARTER + r) * P2T + c] for c in range(P2T)], axis=1)
            for r in range(QUARTER)
        ],
        axis=0,
    )


def placed_two(tab, which, first, second, over):
    parts = [
        (first, 0, N_TWO_A),
        (second, 0, N_TWO_B),
        (over, N_COUP - N_MAIN, N_TWO - N_TWO_A - N_TWO_B),
    ]
    return lambda n: choose(tab[Q_PLACE + which * N_TWO + n], parts)


def quarter_panel(tab, block, coup, parts, quarter):
    rows = []
    for r in range(QUARTER):
        fill = Q_FILL + (quarter * QUARTER + r) * P2T
        rows.append(
            jnp.concatenate(
                [coup(r * P2T + c) * tab[fill + c].astype(F32) for c in range(P2T)], axis=1
            )
        )
    block = block + jnp.concatenate(rows, axis=0)
    lane = lax.broadcasted_iota(jnp.int32, block.shape, 1)
    block = jnp.where(lane < tab[Q_LIVE] * TILE, block, 0.0)
    return times_inverse(block, parts)


WIDE = QUARTER * TILE


def fetch(pairs, sems):
    copies = [pltpu.make_async_copy(src, dst, sems.at[n]) for n, (src, dst) in enumerate(pairs)]
    for c in copies:
        c.start()
    return copies


def rows_kernel(
    tab, part, oth1, high_in, low_in, coup0_in, coup1_a_in, coup1_b_in, over_in, coup2_in,
    panel_out, schur_out, rest_out,
    g, oth, high, low, coup0, coup1_a, coup1_b, over, coup2, other, panels, sems,
):
    copies = fetch(
        [
            (oth1, oth),
            (part.at[pl.ds(G_COUP, G_NONE - G_COUP)], g),
            (coup0_in, coup0),
            (high_in, high),
            (low_in, low),
            (coup1_a_in, coup1_a),
            (coup1_b_in, coup1_b),
            (over_in, over),
            (coup2_in, coup2),
        ],
        sems,
    )
    copies[0].wait()
    get_own(oth, other)
    copies[1].wait()
    extend_two(tab, other, g, 1, HALF_U, HALF_U, True, G_COUP, G_NONE)
    rest_out[...] = quarter_rows_of(tab, g, tab[Q_MINE + 3])
    for c in copies[2:]:
        c.wait()
    parts = high[...], low[...]
    whole = [lambda n, ref=ref: ref[n] for ref in (coup0, coup2)]
    for s, coup in enumerate((whole[0], placed_two(tab, 0, coup1_a, coup1_b, over), whole[1])):
        quarter = tab[Q_MINE + s]
        panel = quarter_panel(tab, quarter_rows_of(tab, g, quarter), coup, parts, quarter)
        panels[s] = panel
        if s == 0:
            panel_out[...] = panel
    left = split(panel_out[...])
    for s in range(4):
        quarter = tab[Q_MINE + s]
        if s < 3:
            product = dot3(left, split(panels[s]), NT)
        for r in range(QUARTER):
            for c in range(QUARTER):
                tile = g[G_TRAIL - G_COUP + r * U2T + quarter * QUARTER + c]
                if s < 3:
                    tile = tile - product[r * TILE : (r + 1) * TILE, c * TILE : (c + 1) * TILE]
                col = pl.multiple_of((quarter * QUARTER + c) * TILE, TILE)
                schur_out[r * TILE : (r + 1) * TILE, pl.ds(col, TILE)] = tile


def last_kernel(
    tab, schur, rest_in, panel_in, high_in, low_in, coup_a_in, coup_b_in, over_in,
    out,
    block, rest, panel, high, low, coup_a, coup_b, over, sems, sem,
):
    quarter = tab[Q_MINE + 3]
    col = pl.ds(pl.multiple_of(quarter * WIDE, TILE), WIDE)
    copies = fetch(
        [
            (rest_in, rest),
            (coup_a_in, coup_a),
            (coup_b_in, coup_b),
            (over_in, over),
            (high_in, high),
            (low_in, low),
            (panel_in, panel),
            (schur.at[:, col], block),
        ],
        sems,
    )
    for c in copies[:6]:
        c.wait()
    coup = placed_two(tab, 1, coup_a, coup_b, over)
    other = quarter_panel(tab, rest[...], coup, (high[...], low[...]), quarter)
    for c in copies[6:]:
        c.wait()
    block[...] = block[...] - dot3(split(panel[...]), split(other), NT)
    leave = pltpu.make_async_copy(block, out.at[:, col], sem)
    leave.start()
    leave.wait()


def swap(array, axis):
    size = lax.axis_size(axis)
    return lax.ppermute(array, axis, [(i, i ^ (size // 2)) for i in range(size)])


def tiles(count):
    return jax.ShapeDtypeStruct((count, TILE, TILE), F32)


def halved(rows):
    return jax.ShapeDtypeStruct((rows, PIVOT), jnp.bfloat16)


def dense(rows, cols):
    return jax.ShapeDtypeStruct((rows, cols), F32)


SMEM = pl.BlockSpec(memory_space=pltpu.SMEM)
VMEM = pl.BlockSpec(memory_space=pltpu.VMEM)
HBM = pl.BlockSpec(memory_space=pl.ANY)
LIMIT = 60 << 20
CHEAP = pl.CostEstimate(flops=1, bytes_accessed=1, transcendentals=0)


def call(kernel, name, out_shape, in_specs, out_specs, scratch=(), waits=(), limit=LIMIT, **options):
    count = len(in_specs)

    def body(*refs):
        kernel(*refs[:count], *refs[count + len(waits) :])

    run = pl.pallas_call(
        body,
        out_shape=out_shape,
        in_specs=in_specs + [HBM] * len(waits),
        out_specs=out_specs,
        scratch_shapes=list(scratch),
        name=name,
        compiler_params=pltpu.CompilerParams(vmem_limit_bytes=limit),
        cost_estimate=CHEAP,
        **options,
    )
    return lambda *args: run(*args, *waits)


def tri(i, k):
    return i * (i + 1) // 2 + k


def local_order(second_map, side):
    unit = jnp.arange(U1T, dtype=jnp.int32)
    rank = second_map + jnp.where(unit // HALF_U == side, 0, P2T + U2T)
    place = jnp.sum((rank[None, :] < rank[:, None]).astype(jnp.int32), axis=1)
    hit = (place[None, :] == unit[:, None]).astype(jnp.int32)
    return place, hit


def place_of(child_map, place):
    unit = jnp.arange(U1T, dtype=jnp.int32)
    hit = (child_map[:, None] - P1T == unit[None, :]).astype(jnp.int32)
    return jnp.where(child_map < P1T, child_map, P1T + jnp.sum(hit * place[None, :], axis=1))


def sort_by(key):
    spot = jnp.sum((key[None, :] < key[:, None]).astype(jnp.int32), axis=1)
    hit = (spot[None, :] == jnp.arange(CT, dtype=jnp.int32)[:, None]).astype(jnp.int32)
    order = jnp.sum(hit * jnp.arange(CT, dtype=jnp.int32)[None, :], axis=1)
    return order, jnp.sum(hit * key[None, :], axis=1)


def turned_key(key):
    return jnp.where(key < P1T, key, P1T + (key - P1T + HALF_U) % U1T)


def slots(keys):
    row = keys[:, None]
    col = keys[None, :]
    own = P1T + HALF_U
    pivot = row * P1T + col
    coup = jnp.where(row >= own, S_COUP + (row - own) * P1T, S_FAR + (row - P1T) * P1T) + col
    near = S_OWN + tri(row - own, col - own)
    cross = S_CROSS + (row - own) * HALF_U + col - P1T
    other = S_OTH + tri(row - P1T, col - P1T)
    rest = jnp.where(row < own, other, jnp.where(col < own, cross, near))
    return jnp.where(row < P1T, pivot, jnp.where(col < P1T, coup, rest)).reshape(-1)


def needed_first(need):
    need = need.reshape(-1)
    count = need.shape[0]
    at = jnp.arange(count, dtype=jnp.int32)
    key = at + jnp.where(need > 0, 0, count)
    place = jnp.sum((key[None, :] < key[:, None]).astype(jnp.int32), axis=1)
    order = jnp.sum((place[None, :] == at[:, None]).astype(jnp.int32) * at[None, :], axis=1)
    return place, order


def needed(fill, live):
    return fill * (jnp.arange(fill.shape[-1], dtype=jnp.int32) < live[..., None, None])


def targets(goal, quarter):
    row = goal[:, None]
    col = goal[None, :]

    def index(r, c):
        mine = (r - P2T) // QUARTER == quarter
        coup = G_COUP + (r - P2T) * P2T + c
        trail = G_TRAIL + (r - P2T - quarter * QUARTER) * U2T + c - P2T
        rest = jnp.where(c < P2T, coup, jnp.where(mine, trail, G_NONE))
        return jnp.where(r < P2T, jnp.where((c < P2T) & (r >= c), r * P2T + c, G_NONE), rest)

    direct = index(row, col)
    turned = jnp.where(row == col, G_NONE, index(col, row))
    return direct.reshape(-1), turned.reshape(-1)


def body(
    contribution,
    pivot_one,
    rows_one,
    pivot_two,
    rows_two,
    map_one,
    map_two,
    fill_one,
    fill_two,
    live_one,
    live_two,
):
    size_lo = lax.axis_size("lo")
    size_hi = lax.axis_size("hi")
    half_lo = size_lo // 2
    half_hi = size_hi // 2
    index_lo = lax.axis_index("lo")
    index_hi = lax.axis_index("hi")
    side_lo = index_lo // half_lo
    side_hi = index_hi // half_hi
    front_lo = index_lo % half_lo
    front_hi = index_hi % half_hi
    far_lo = (index_lo + half_lo) % size_lo
    far_hi = (index_hi + half_hi) % size_hi
    quarter = 2 * side_hi + side_lo
    block, pivot, rows = contribution[0, 0], pivot_one[0, 0], rows_one[0, 0]
    pivot_second, rows_second = pivot_two[0, 0], rows_two[0, 0]

    second_map = map_two[index_hi, front_lo]
    place, hit = local_order(second_map, side_lo)
    key = place_of(map_one[index_hi, index_lo], place)
    order_sent, _ = sort_by(key)
    tab_first = jnp.concatenate([order_sent, side_lo[None]]).astype(jnp.int32)
    sent = call(
        pack_first,
        "pack_first",
        dense(N_FIRST * TILE + ROWS, TILE),
        [SMEM, HBM, HBM],
        VMEM,
        [
            pltpu.VMEM((DIAG_FIRST, TILE, TILE), F32),
            pltpu.SemaphoreType.DMA((len(TRI_C) + len(TRI_P),)),
        ],
    )(tab_first, block, pivot)
    got_first = swap(sent, "lo")

    unit = jnp.arange(U1T, dtype=jnp.int32)
    local = jnp.sum(hit * unit[None, :], axis=1)
    order_kept, keys = sort_by(turned_key(key))
    live_first = live_one[index_hi, front_lo]
    need_first = needed(
        jnp.sum(hit[:, :, None] * fill_one[index_hi, front_lo][None, :, :], axis=1), live_first
    )
    live_second = live_two[front_hi, front_lo]
    need_second = needed(fill_two[front_hi, front_lo], live_second)

    def place_second(which):
        return needed_first(
            lax.dynamic_slice_in_dim(need_second, which * QUARTER, QUARTER, 0)
        )

    _, order_main = needed_first(need_first[:HALF_U])
    _, order_two = place_second(quarter)
    tab_rest = jnp.concatenate(
        [tab_first, order_kept, local, quarter[None], order_main, order_two]
    ).astype(jnp.int32)
    shapes = [
        tiles(N_COUP), tiles(N_TRI), tiles(len(TRI_C)), tiles(N_CROSS), tiles(N_OFF + len(TRI_P)),
        tiles(N_TWO),
        dense(N_WIDE * HALF, TILE), dense(N_WIDE * HALF, TILE),
        tiles(N_MAIN), tiles(N_TWO_A), tiles(N_TWO_B), tiles(N_OVER),
    ]
    n_rest = 2 * N_COUP + N_TRI + len(TRI_C) + N_CROSS + N_OFF + len(TRI_P) + 2 * N_TWO + N_UNIT
    coup, own, kept, cross, off, two, units, units_sent, main, two_a, two_b, over = call(
        pack_rest,
        "pack_rest",
        shapes,
        [SMEM] + [HBM] * 5,
        [VMEM] * len(shapes),
        [pltpu.VMEM((N_UNIT, HALF, TILE), F32), pltpu.SemaphoreType.DMA((n_rest,))],
        waits=(sent,),
    )(tab_rest, block, pivot, rows, pivot_second, rows_second)
    two_hi = swap(two, "hi")
    units_hi = swap(units, "hi")
    far_key = place_of(map_one[index_hi, far_lo], place)
    _, far_keys = sort_by(turned_key(far_key))
    place_main, _ = needed_first(need_first[HALF_U:])
    tab_one = jnp.concatenate(
        [side_lo[None], live_first[None], local, need_first.reshape(-1), slots(keys), slots(far_keys), place_main]
    ).astype(jnp.int32)
    map_far = map_two[far_hi, front_lo]
    _, hit_far = local_order(map_far, side_lo)
    direct, turned = targets(jnp.sum(hit * second_map[None, :], axis=1), quarter)
    direct_far, turned_far = targets(jnp.sum(hit_far * map_far[None, :], axis=1), quarter)
    place_lo, _ = place_second(2 * side_hi + 1 - side_lo)
    place_both, _ = place_second(2 * (1 - side_hi) + 1 - side_lo)
    quarters = jnp.stack(
        [quarter, 2 * side_hi + 1 - side_lo, 2 * (1 - side_hi) + side_lo, 2 * (1 - side_hi) + 1 - side_lo]
    )
    tab_two = jnp.concatenate(
        [
            live_second[None], quarters, need_second.reshape(-1),
            direct, direct_far, turned, turned_far, place_lo, place_both,
        ]
    ).astype(jnp.int32)
    most = jnp.max(jnp.sum(needed(fill_one, live_one).reshape(-1, N_COUP), axis=1))
    most_two = jnp.max(jnp.sum(needed(fill_two, live_two).reshape(-1, N_TWO), axis=1))

    def send_over(array):
        got = swap(array, "lo")
        return got, swap(got, "hi")

    over_got, over_both = lax.cond(
        (most > N_MAIN) | (most_two > N_TWO_A + N_TWO_B),
        send_over,
        lambda array: (array, array),
        over,
    )
    main = after(main, part_of(got_first), two_hi, units_hi, tab_one, tab_two, over_got, over_both)
    got_main = swap(main, "lo")

    half_rows = HALF_U * TILE
    message = dense(N_OWN * TILE + ROWS, TILE)
    lower_one, inv_a, inv_b, panel_a, panel_b, panel_one, s_own, own_sent, far_part = call(
        first_kernel,
        "first_front_own",
        [
            dense(PIVOT // 2, PIVOT), *[halved(PIVOT)] * 2, *[halved(half_rows)] * 2,
            dense(half_rows, PIVOT), message, message, tiles(N_CROSS + N_COUP),
        ],
        [SMEM] + [VMEM] * 6,
        [VMEM] * 8 + [HBM],
        [
            pltpu.VMEM((N_FRONT, TILE, TILE), F32),
            pltpu.VMEM((PIVOT, PIVOT), F32),
            pltpu.VMEM((PIVOT, PIVOT), F32),
            pltpu.VMEM((PIVOT, PIVOT), F32),
            pltpu.SemaphoreType.DMA,
        ],
    )(tab_one, kept, got_first, coup, own, cross, off)
    s_own_far = swap(s_own, "hi")
    block = pltpu.VMEM((N_TRI, TILE, TILE), F32)
    part = call(third_kernel, "second_front_part", tiles(G_NONE), [SMEM] + [VMEM] * 4, VMEM, [block])(
        tab_two, s_own, units, units_hi, rows_second
    )
    own_sent = after(own_sent, part_of(got_main), part)
    got_own = swap(own_sent, "lo")


    def cross_of(which, *waits):
        return call(
            functools.partial(second_kernel, which),
            "first_front_other",
            tiles(N_CROSS_A),
            [SMEM, HBM] + [VMEM] * 6,
            VMEM,
            [
                pltpu.VMEM((N_COUP // 2, TILE, TILE), F32),
                pltpu.VMEM((N_CROSS_A, TILE, TILE), F32),
                pltpu.SemaphoreType.DMA((1 + HALF_U,)),
            ],
            waits=waits,
        )(tab_one, far_part, got_main, over_got, inv_a, inv_b, panel_a, panel_b)

    cross_a = cross_of(0, s_own_far, own_sent)
    cross_a_far = swap(cross_a, "hi")
    cross_b = cross_of(1, cross_a)
    cross_b_far = swap(cross_b, "hi")
    got_units = swap(after(units_sent, got_own), "lo")
    s_oth_far = swap(got_own, "hi")
    units_both = swap(got_units, "hi")
    got_two_a = swap(after(two_a, got_units, cross_a_far, cross_b_far), "lo")
    part = call(
        more_kernel,
        "second_front_more",
        tiles(G_NONE),
        [SMEM, HBM] + [VMEM] * 7,
        VMEM,
        [block, pltpu.SemaphoreType.DMA],
    )(tab_two, part, s_own_far, cross_a, cross_b, cross_a_far, cross_b_far, got_own, got_units)
    two_b = after(two_b, got_two_a, units_both, s_oth_far, part)
    got_two_b = swap(two_b, "lo")
    two_a_both = swap(got_two_a, "hi")
    half = jax.ShapeDtypeStruct((SECOND, SECOND), jnp.bfloat16)
    square = pltpu.VMEM((SECOND, SECOND), F32)
    lower_two, inv_high, inv_low = call(
        pivot_kernel,
        "second_front_pivot",
        [dense(SECOND // 4, SECOND), half, half],
        [SMEM, HBM] + [VMEM] * 2,
        [VMEM] * 3,
        [
            pltpu.VMEM((G_COUP, TILE, TILE), F32),
            pltpu.VMEM((N_TRI, TILE, TILE), F32),
            square, square, square,
            pltpu.SemaphoreType.DMA,
        ],
        waits=(two_b,),
    )(tab_two, part, s_oth_far, units_both)
    got_two_b = after(got_two_b, lower_two, two_a_both)
    two_b_both = swap(got_two_b, "hi")
    rows_wide = pltpu.VMEM((WIDE, SECOND), F32)
    halves = [pltpu.VMEM((SECOND, SECOND), jnp.bfloat16)] * 2
    sent_two = [pltpu.VMEM((n, TILE, TILE), F32) for n in (N_TWO_A, N_TWO_B, N_OVER)]
    whole_two = pltpu.VMEM((N_TWO, TILE, TILE), F32)
    panel_two, schur, rest = call(
        rows_kernel,
        "second_front_rows",
        [dense(WIDE, SECOND), dense(WIDE, U2T * TILE), dense(WIDE, SECOND)],
        [SMEM] + [HBM] * 9,
        [VMEM] * 3,
        [
            pltpu.VMEM((G_NONE - G_COUP, TILE, TILE), F32),
            pltpu.VMEM((N_OWN * TILE + ROWS, TILE), F32),
            *halves,
            whole_two,
            *sent_two,
            whole_two,
            block,
            pltpu.VMEM((3, WIDE, SECOND), F32),
            pltpu.SemaphoreType.DMA((9,)),
        ],
    )(tab_two, part, s_oth_far, inv_high, inv_low, two, got_two_a, got_two_b, over_got, two_hi)
    schur_two = call(
        last_kernel,
        "second_front_last",
        dense(WIDE, U2T * TILE),
        [SMEM] + [HBM] * 8,
        HBM,
        [
            pltpu.VMEM((WIDE, WIDE), F32),
            rows_wide,
            rows_wide,
            *halves,
            *sent_two,
            pltpu.SemaphoreType.DMA((8,)),
            pltpu.SemaphoreType.DMA,
        ],
        input_output_aliases={1: 0},
    )(tab_two, schur, rest, panel_two, inv_high, inv_low, two_a_both, two_b_both, over_both)
    return (
        lower_one[None, None],
        panel_one[None, None],
        lower_two[None, None],
        panel_two[None, None],
        schur_two[None, None],
    )


def solution(mesh):
    split_both = P("hi", "lo", None, None)
    return jax.shard_map(
        body,
        mesh=mesh,
        in_specs=(split_both,) * 5 + (P(),) * 6,
        out_specs=(split_both,) * 5,
        check_vma=False,
    )
```

profile of v0, /device:TPU:0, one launch (start us, length us, event | category | flops | bytes accessed | tf_op | source)
XLA Modules:
  0.0 371.0 jit_solution(1034709942066106387)
XLA Ops:
  0.7 0.7 fusion.23
  1.6 0.8 broadcast_add_fusion.15
  2.6 0.8 compare_select_fusion.2
  3.9 0.6 pad_add_fusion.refs_0_
  4.5 4.5 %pack_first.1.refs_6_ = f32[4744,128]{1,0:T(8,128)} custom-call(s32[9]{0:T(128)} %pad_add_fusion.refs_0_, f32[1024,1024]{1,0:T(8,128)} %bitcast.47, f32[384,768]{1,0:T(8,128)} %bitcast.52), custom_call_target="tpu_custom_call" | custom-call | flops 1 | bytes 1 | tf_op jit(solution)/shard_map/pack_first/pallas_call | solution.py:824
  9.0 4.1 %collective-permute-start.2 = (f32[4744,128]{1,0:T(8,128)}, f32[4744,128]{1,0:T(8,128)}, u32[]{:S(2)}, u32[]{:S(2)}) collective-permute-start(f32[4744,128]{1,0:T(8,128)} %pack_first.1.refs_6_), channel_id=1, source_target_pairs={{0,16},{4,20},{8,24},{12,28},{16,0},{20,4},{24,8},{28,12},{1,17},{... | collective-permute-start | bytes 7286792 | tf_op jit(solution)/shard_map/ppermute | solution.py:785
  13.1 0.6 dynamic_slice.33
  13.8 0.7 compare_convert_fusion.1
  15.2 0.6 dynamic_slice.39
  17.0 0.7 concatenate.14.refs_0_
  17.7 13.5 %pack_rest.1 = (f32[36,128,128]{2,1,0:T(8,128)}, f32[21,128,128]{2,1,0:T(8,128)}, f32[36,128,128]{2,1,0:T(8,128)}, f32[36,128,128]{2,1,0:T(8,128)}, f32[15,128,1...) custom-call(s32[84]{0:T(128)} %concatenate.14.refs_0_, ...), custom_call_target="tpu_custom_call" | custom-call | flops 1 | bytes 1 | tf_op jit(solution)/shard_map/pack_rest/pallas_call | solution.py:824
  31.1 1.6 collective-permute-start.3
  38.5 0.7 reduce_max.18
  39.2 0.7 reduce_max.19
  41.3 0.8 conditional.1
  41.3 0.8 copy.55
  42.1 1.3 concatenate.13.refs_0_.refs_4_
  43.6 1.2 concatenate.16.refs_0_.refs_5_
  44.8 73.3 %collective-permute-done.2.refs_2_ = f32[4744,128]{1,0:T(8,128)} collective-permute-done((f32[4744,128]{1,0:T(8,128)}, f32[4744,128]{1,0:T(8,128)}, u32[]{:S(2)}, u32[]{:S(2)}) %collective-permute-start.2) | collective-permute-done | bytes 2428960 | tf_op jit(solution)/shard_map/ppermute | solution.py:785
  118.2 1.3 slice.24.refs_1_
  119.5 0.7 copy-done.6
  120.6 57.1 %first_front_own.1 = (f32[384,768]{1,0:T(8,128)}, bf16[768,768]{1,0:T(8,128)(2,1)}, bf16[768,768]{1,0:T(8,128)(2,1)}, bf16[768,768]{1,0:T(8,128)(2,1)}, bf16[768...) custom-call(s32[250]{0:T(256)} %concatenate.13.refs_0_.refs_4_, ...), custom_call_target="tpu_custom_call" | custom-call | flops 1 | bytes 1 | tf_op jit(solution)/shard_map/first_front_own/pallas_call | solution.py:824
  177.7 1.6 collective-permute-start.4
  179.3 12.2 %second_front_part.1.refs_2_.refs_1_ = f32[144,128,128]{2,1,0:T(8,128)} custom-call(s32[689]{0:T(1024)} %concatenate.16.refs_0_.refs_5_, f32[2312,128]{1,0:T(8,128)} %get-tuple-element.43.refs_1_, f32[704,128]{1,0:T(8,128)} %get-tuple-element.44.refs_2_, f32[704,128]{1,0:T(8,128)} %copy-done.6, f32[384,2304]{1,0:T(8,128)} %bitcast.50), custom_call_target="tpu_custom_call" | custom-call | flops 1 | bytes 1 | tf_op jit(solution)/shard_map/second_front_part/pallas_call | solution.py:824
  191.5 16.4 %collective-permute-done.6.refs_2_ = f32[30,128,128]{2,1,0:T(8,128)S(1)} collective-permute-done((f32[30,128,128]{2,1,0:T(8,128)}, f32[30,128,128]{2,1,0:T(8,128)S(1)}, u32[]{:S(2)}, u32[]{:S(2)}) %collective-permute-start.6) | collective-permute-done | bytes 1966112 | tf_op jit(solution)/shard_map/ppermute | solution.py:785
  207.8 0.6 slice_bitcast_fusion.refs_1_
  208.5 0.6 copy-done.1
  209.1 9.7 %first_front_other.2.refs_8_.refs_3_ = f32[18,128,128]{2,1,0:T(8,128)} custom-call(s32[250]{0:T(256)} %concatenate.13.refs_0_.refs_4_, f32[72,128,128]{2,1,0:T(8,128)} %get-tuple-element.45.refs_1_, f32[30,128,128]{2,1,0:T(8,128)} %copy-done.1, f32[8,128,128]{2,1,0:T(8,128)S(1)} %get-tuple-element.49.refs_6_.refs_3_.refs_8_, ...), custom_call_target="tpu_custom_call" | custom-call | flops 1 | bytes 1 | tf_op jit(solution)/shard_map/first_front_other/pallas_call | solution.py:824
  218.8 1.3 collective-permute-start.7
  220.1 9.7 %first_front_other.3.refs_4_ = f32[18,128,128]{2,1,0:T(8,128)} custom-call(s32[250]{0:T(256)} %concatenate.13.refs_0_.refs_4_, f32[72,128,128]{2,1,0:T(8,128)} %get-tuple-element.45.refs_1_, f32[30,128,128]{2,1,0:T(8,128)} %copy-done.1, f32[8,128,128]{2,1,0:T(8,128)S(1)} %get-tuple-element.49.refs_6_.refs_3_.refs_8_, ...), custom_call_target="tpu_custom_call" | custom-call | flops 1 | bytes 1 | tf_op jit(solution)/shard_map/first_front_other/pallas_call | solution.py:824
  229.8 0.8 collective-permute-start.8
  230.7 31.3 %collective-permute-done.9.refs_1_.refs_7_ = f32[2312,128]{1,0:T(8,128)} collective-permute-done((f32[2312,128]{1,0:T(8,128)}, f32[2312,128]{1,0:T(8,128)}, u32[]{:S(2)}, u32[]{:S(2)}) %collective-permute-start.9) | collective-permute-done | bytes 1183776 | tf_op jit(solution)/shard_map/ppermute | solution.py:785
  262.0 0.9 collective-permute-start.11
  263.0 17.5 %collective-permute-done.10.refs_8_.refs_1_ = f32[704,128]{1,0:T(8,128)} collective-permute-done((f32[704,128]{1,0:T(8,128)}, f32[704,128]{1,0:T(8,128)}, u32[]{:S(2)}, u32[]{:S(2)}) %collective-permute-start.10) | collective-permute-done | bytes 360480 | tf_op jit(solution)/shard_map/ppermute | solution.py:785
  280.5 1.1 collective-permute-start.12
  281.6 1.0 copy-done.2
  282.6 19.1 %second_front_more.1.refs_4_.refs_1_ = f32[144,128,128]{2,1,0:T(8,128)} custom-call(s32[689]{0:T(1024)} %concatenate.16.refs_0_.refs_5_, f32[144,128,128]{2,1,0:T(8,128)} %second_front_part.1.refs_2_.refs_1_, f32[2312,128]{1,0:T(8,128)} %collective-permute-done.4.refs_8_.refs_2_, f32[18,128,128]{2,1,0:T(8,128)} %first_front_other.2.refs_8_.refs_3_, ...), custom_call_target="tpu_custom_call" | custom-call | flops 1 | bytes 1 | tf_op jit(solution)/shard_map/second_front_more/pallas_call | solution.py:824
  301.7 2.0 collective-permute-done.12.refs_2_.refs_3_
  303.7 0.7 copy-done.5
  304.8 2.6 collective-permute-start.14
  307.5 0.9 collective-permute-start.15
  308.4 36.9 %second_front_pivot.1 = (f32[192,768]{1,0:T(8,128)}, bf16[768,768]{1,0:T(8,128)(2,1)}, bf16[768,768]{1,0:T(8,128)(2,1)}) custom-call(s32[689]{0:T(1024)} %concatenate.16.refs_0_.refs_5_, f32[144,128,128]{2,1,0:T(8,128)} %second_front_more.1.refs_4_.refs_1_, f32[2312,128]{1,0:T(8,128)} %copy-done, f32[704,128]{1,0:T(8,128)} %copy-done.5, ...), custom_call_target="tpu_custom_call" | custom-call | flops 1 | bytes 1 | tf_op jit(solution)/shard_map/second_front_pivot/pallas_call | solution.py:824
  345.4 0.7 copy-done.7
  346.4 1.1 collective-permute-start.16
  347.5 13.7 %second_front_rows.1 = (f32[384,768]{1,0:T(8,128)}, f32[384,1536]{1,0:T(8,128)}, f32[384,768]{1,0:T(8,128)}) custom-call(s32[689]{0:T(1024)} %concatenate.16.refs_0_.refs_5_, f32[144,128,128]{2,1,0:T(8,128)} %second_front_more.1.refs_4_.refs_1_, f32[2312,128]{1,0:T(8,128)} %copy-done, bf16[768,768]{1,0:T(8,128)(2,1)} %get-tuple-element.60.refs_3_.refs_4_, ...), custom_call_target="tpu_custom_call" | custom-call | flops 1 | bytes 1 | tf_op jit(solution)/shard_map/second_front_rows/pallas_call | solution.py:824
  361.2 0.7 collective-permute-done.16.refs_7_
  361.9 0.9 copy-done.9
  362.8 8.1 %second_front_last.1 = f32[384,1536]{1,0:T(8,128)} custom-call(s32[689]{0:T(1024)} %concatenate.16.refs_0_.refs_5_, f32[384,1536]{1,0:T(8,128)} %get-tuple-element.63.refs_1_, f32[384,768]{1,0:T(8,128)} %get-tuple-element.64.refs_2_, f32[384,768]{1,0:T(8,128)} %get-tuple-element.62.refs_3_, ...), custom_call_target="tpu_custom_call", output_to_operand_aliasing={{}: (1, {})} | custom-call | flops 1 | bytes 1 | tf_op jit(solution)/shard_map/second_front_last/pallas_call | solution.py:824
  (137 shorter events, 9.8 us)
Async XLA Ops:
  4.5 8.6 %copy-start.12 = (s32[4,4]{1,0:T(4,128)S(1)}, s32[4,4]{1,0:T(4,128)}, u32[]{:S(2)}) copy-start(s32[4,4]{1,0:T(4,128)} %param.22) | copy-start | bytes 196
  4.5 9.3 %copy-start.10 = (s32[4,4,12,6]{2,1,3,0:T(4,128)S(1)}, s32[4,4,12,6]{2,1,3,0:T(4,128)}, u32[]{:S(2)}) copy-start(s32[4,4,12,6]{2,1,3,0:T(4,128)} %param.20) | copy-start | bytes 13828
  4.5 9.3 %copy-start.11 = (s32[2,4,12,6]{2,1,3,0:T(4,128)S(1)}, s32[2,4,12,6]{2,1,3,0:T(4,128)}, u32[]{:S(2)}) copy-start(s32[2,4,12,6]{2,1,3,0:T(4,128)} %param.21) | copy-start | bytes 6916
  4.5 10.7 %copy-start.13 = (s32[2,4]{1,0:T(2,128)S(1)}, s32[2,4]{1,0:T(2,128)}, u32[]{:S(2)}) copy-start(s32[2,4]{1,0:T(2,128)} %param.23) | copy-start | bytes 100
  9.0 109.2 %collective-permute-start.2 = (f32[4744,128]{1,0:T(8,128)}, f32[4744,128]{1,0:T(8,128)}, u32[]{:S(2)}, u32[]{:S(2)}) collective-permute-start(f32[4744,128]{1,0:T(8,128)} %pack_first.1.refs_6_), channel_id=1, source_target_pairs={{0,16},{4,20},{8,24},{12,28},{16,0},{20,4},{24,8},{28,12},{1,17},{... | collective-permute-start | bytes 7286792 | tf_op jit(solution)/shard_map/ppermute | solution.py:785
  31.1 88.3 %collective-permute-start.3 = (f32[704,128]{1,0:T(8,128)}, f32[704,128]{1,0:T(8,128)S(1)}, u32[]{:S(2)}, u32[]{:S(2)}) collective-permute-start(f32[704,128]{1,0:T(8,128)} %get-tuple-element.44.refs_2_), channel_id=1, source_target_pairs={{0,2},{1,3},{2,0},{3,1},{4,6},{5,7},{6,4},{7,5},{8,10},{9,11},{10,... | collective-permute-start | bytes 1081352 | tf_op jit(solution)/shard_map/ppermute | solution.py:785
  32.7 86.7 %collective-permute-start.5 = (f32[18,128,128]{2,1,0:T(8,128)}, f32[18,128,128]{2,1,0:T(8,128)S(1)}, u32[]{:S(2)}, u32[]{:S(2)}) collective-permute-start(f32[18,128,128]{2,1,0:T(8,128)} %get-tuple-element.47.refs_5_), channel_id=1, source_target_pairs={{0,2},{1,3},{2,0},{3,1},{4,6},{5,7},{6,4},{7,5},{8,10},{9,11},{10,... | collective-permute-start | bytes 3538952 | tf_op jit(solution)/shard_map/ppermute | solution.py:785
  119.4 0.8 copy-start.6
  119.4 1.1 copy-start.3
  120.6 87.2 %collective-permute-start.6 = (f32[30,128,128]{2,1,0:T(8,128)}, f32[30,128,128]{2,1,0:T(8,128)S(1)}, u32[]{:S(2)}, u32[]{:S(2)}) collective-permute-start(f32[30,128,128]{2,1,0:T(8,128)} %after.6), channel_id=1, source_target_pairs={{0,16},{4,20},{8,24},{12,28},{16,0},{20,4},{24,8},{28,12},{1,17},{... | collective-permute-start | bytes 5898248 | tf_op jit(solution)/shard_map/ppermute | solution.py:785
  177.7 31.4 %collective-permute-start.4 = (f32[2312,128]{1,0:T(8,128)}, f32[2312,128]{1,0:T(8,128)}, u32[]{:S(2)}, u32[]{:S(2)}) collective-permute-start(f32[2312,128]{1,0:T(8,128)} %get-tuple-element.43.refs_1_), channel_id=1, source_target_pairs={{0,2},{1,3},{2,0},{3,1},{4,6},{5,7},{6,4},{7,5},{8,10},{9,11},{10,... | collective-permute-start | bytes 3551240 | tf_op jit(solution)/shard_map/ppermute | solution.py:785
  207.8 1.3 copy-start.1
  209.1 52.9 %collective-permute-start.9 = (f32[2312,128]{1,0:T(8,128)}, f32[2312,128]{1,0:T(8,128)}, u32[]{:S(2)}, u32[]{:S(2)}) collective-permute-start(f32[2312,128]{1,0:T(8,128)} %after.7.refs_9_), channel_id=1, source_target_pairs={{0,16},{4,20},{8,24},{12,28},{16,0},{20,4},{24,8},{28,12},{1,17},{... | collective-permute-start | bytes 3551240 | tf_op jit(solution)/shard_map/ppermute | solution.py:785
  218.8 62.8 %collective-permute-start.7 = (f32[18,128,128]{2,1,0:T(8,128)}, f32[18,128,128]{2,1,0:T(8,128)S(1)}, u32[]{:S(2)}, u32[]{:S(2)}) collective-permute-start(f32[18,128,128]{2,1,0:T(8,128)} %first_front_other.2.refs_8_.refs_3_), channel_id=1, source_target_pairs={{0,2},{1,3},{2,0},{3,1},{4,6},{5,7},{6,4},{7,5},{8,10},{9,11},{10,... | collective-permute-start | bytes 3538952 | tf_op jit(solution)/shard_map/ppermute | solution.py:785
  229.8 51.8 %collective-permute-start.8 = (f32[18,128,128]{2,1,0:T(8,128)}, f32[18,128,128]{2,1,0:T(8,128)}, u32[]{:S(2)}, u32[]{:S(2)}) collective-permute-start(f32[18,128,128]{2,1,0:T(8,128)} %first_front_other.3.refs_4_), channel_id=1, source_target_pairs={{0,2},{1,3},{2,0},{3,1},{4,6},{5,7},{6,4},{7,5},{8,10},{9,11},{10,... | collective-permute-start | bytes 3538952 | tf_op jit(solution)/shard_map/ppermute | solution.py:785
  262.0 41.7 %collective-permute-start.11 = (f32[2312,128]{1,0:T(8,128)}, f32[2312,128]{1,0:T(8,128)S(1)}, u32[]{:S(2)}, u32[]{:S(2)}) collective-permute-start(f32[2312,128]{1,0:T(8,128)} %collective-permute-done.9.refs_1_.refs_7_), channel_id=1, source_target_pairs={{0,2},{1,3},{2,0},{3,1},{4,6},{5,7},{6,4},{7,5},{8,10},{9,11},{10,... | collective-permute-start | bytes 3551240 | tf_op jit(solution)/shard_map/ppermute | solution.py:785
  263.0 17.5 %collective-permute-start.10 = (f32[704,128]{1,0:T(8,128)}, f32[704,128]{1,0:T(8,128)}, u32[]{:S(2)}, u32[]{:S(2)}) collective-permute-start(f32[704,128]{1,0:T(8,128)} %after.8), channel_id=1, source_target_pairs={{0,16},{4,20},{8,24},{12,28},{16,0},{20,4},{24,8},{28,12},{1,17},{... | collective-permute-start | bytes 1081352 | tf_op jit(solution)/shard_map/ppermute | solution.py:785
  280.5 23.2 %collective-permute-start.12 = (f32[704,128]{1,0:T(8,128)}, f32[704,128]{1,0:T(8,128)S(1)}, u32[]{:S(2)}, u32[]{:S(2)}) collective-permute-start(f32[704,128]{1,0:T(8,128)} %collective-permute-done.10.refs_8_.refs_1_), channel_id=1, source_target_pairs={{0,2},{1,3},{2,0},{3,1},{4,6},{5,7},{6,4},{7,5},{8,10},{9,11},{10,... | collective-permute-start | bytes 1081352 | tf_op jit(solution)/shard_map/ppermute | solution.py:785
  281.6 1.0 copy-start.2
  282.6 19.1 %collective-permute-start.13 = (f32[5,128,128]{2,1,0:T(8,128)}, f32[5,128,128]{2,1,0:T(8,128)S(1)}, u32[]{:S(2)}, u32[]{:S(2)}) collective-permute-start(f32[5,128,128]{2,1,0:T(8,128)} %after.9), channel_id=1, source_target_pairs={{0,16},{4,20},{8,24},{12,28},{16,0},{20,4},{24,8},{28,12},{1,17},{... | collective-permute-start | bytes 983048 | tf_op jit(solution)/shard_map/ppermute | solution.py:785
  301.7 2.0 copy-start.8
  303.7 0.7 copy-start.5
  303.7 1.1 copy-start
  304.8 40.5 %collective-permute-start.14 = (f32[11,128,128]{2,1,0:T(8,128)}, f32[11,128,128]{2,1,0:T(8,128)S(1)}, u32[]{:S(2)}, u32[]{:S(2)}) collective-permute-start(f32[11,128,128]{2,1,0:T(8,128)} %after.10.refs_4_), channel_id=1, source_target_pairs={{0,16},{4,20},{8,24},{12,28},{16,0},{20,4},{24,8},{28,12},{1,17},{... | collective-permute-start | bytes 2162696 | tf_op jit(solution)/shard_map/ppermute | solution.py:785
  307.5 37.9 %collective-permute-start.15 = (f32[5,128,128]{2,1,0:T(8,128)}, f32[5,128,128]{2,1,0:T(8,128)S(1)}, u32[]{:S(2)}, u32[]{:S(2)}) collective-permute-start(f32[5,128,128]{2,1,0:T(8,128)} %copy-done.8), channel_id=1, source_target_pairs={{0,2},{1,3},{2,0},{3,1},{4,6},{5,7},{6,4},{7,5},{8,10},{9,11},{10,... | collective-permute-start | bytes 983048 | tf_op jit(solution)/shard_map/ppermute | solution.py:785
  345.4 0.7 copy-start.7
  345.4 1.0 copy-start.4
  346.4 15.5 %collective-permute-start.16 = (f32[11,128,128]{2,1,0:T(8,128)}, f32[11,128,128]{2,1,0:T(8,128)S(1)}, u32[]{:S(2)}, u32[]{:S(2)}) collective-permute-start(f32[11,128,128]{2,1,0:T(8,128)} %after.11.refs_7_), channel_id=1, source_target_pairs={{0,2},{1,3},{2,0},{3,1},{4,6},{5,7},{6,4},{7,5},{8,10},{9,11},{10,... | collective-permute-start | bytes 2162696 | tf_op jit(solution)/shard_map/ppermute | solution.py:785
  361.9 0.9 copy-start.9
where the time goes:
time: 376 us; the launch traced here: 371 us
  Pallas kernels  184 us (49%)
  waiting for transfers between devices  141 us (38%)
  starting transfers between devices  16.7 us (4%)
  local copies, waits for them, and re-layouts  16.3 us (4%)
  other arithmetic  9.7 us (3%)
    pallas_call x10, Pallas kernels, call(): return lambda *args: run(*args, *waits)  184 us
    ppermute x15, waiting for transfers between devices, swap(): return lax.ppermute(array, axis, [(i, i ^ size // 2) for i in range(size)])  141 us
    ppermute x15, starting transfers between devices, swap(): return lax.ppermute(array, axis, [(i, i ^ size // 2) for i in range(size)])  16.7 us
  transfers between devices with their start and end apart: 15, of which 6 were waited for; matrix products, arithmetic and copies ran while one was open for 4% of the time, Pallas kernels for 46%

commit v1 on v0

--- a/solution.py
+++ b/solution.py
@@ -46,7 +46,8 @@
 N_TRI = len(TRI_U)
 N_CROSS = HALF_U * HALF_U
 N_CROSS_A = N_CROSS // 2
-N_OVER = N_COUP - N_MAIN + N_TWO - N_TWO_A - N_TWO_B
+N_OVER = N_COUP - N_MAIN
+N_TWO_OVER = N_TWO - N_TWO_A - N_TWO_B
 S_COUP = N_PIV
 S_OWN = S_COUP + N_COUP
 S_FAR = S_OWN + N_TRI
@@ -277,7 +278,7 @@
 def pack_rest(
     tab, block, pivot, rows, pivot_second, second,
     coup, own, kept, cross, off, coup_two, units, units_sent, main, two_sent_a, two_sent_b, over,
-    strips, sems,
+    two_over, strips, sems,
 ):
     side = tab[CT]
     order = CT + 1
@@ -323,7 +324,7 @@
         elif p < N_TWO_A + N_TWO_B:
             sent = two_sent_b.at[p - N_TWO_A]
         else:
-            sent = over.at[p + N_COUP - N_MAIN - N_TWO_A - N_TWO_B]
+            sent = two_over.at[p - N_TWO_A - N_TWO_B]
         pairs.append((tile_at(second, n // P2T, n % P2T), sent))
     far = []
     for i in range(OWN_UNITS):
@@ -510,7 +511,7 @@
 
     def tile_of(r, c):
         n = (which * wide + r) * P1T + c
-        tile = choose(tab[T_PLACE + n], [(main, 0, N_MAIN), (over, 0, N_COUP - N_MAIN)])
+        tile = choose(tab[T_PLACE + n], [(main, 0, N_MAIN), (over, 0, N_OVER)])
         return rows_far[r * P1T + c] + tile * tab[T_FILL + N_COUP + n].astype(F32)
 
     for c in copies:
@@ -670,7 +671,7 @@
     parts = [
         (first, 0, N_TWO_A),
         (second, 0, N_TWO_B),
-        (over, N_COUP - N_MAIN, N_TWO - N_TWO_A - N_TWO_B),
+        (over, 0, N_TWO_OVER),
     ]
     return lambda n: choose(tab[Q_PLACE + which * N_TWO + n], parts)
 
@@ -968,9 +969,10 @@
         tiles(N_TWO),
         dense(N_WIDE * HALF, TILE), dense(N_WIDE * HALF, TILE),
         tiles(N_MAIN), tiles(N_TWO_A), tiles(N_TWO_B), tiles(N_OVER),
+        tiles(N_TWO_OVER),
     ]
     n_rest = 2 * N_COUP + N_TRI + len(TRI_C) + N_CROSS + N_OFF + len(TRI_P) + 2 * N_TWO + N_UNIT
-    coup, own, kept, cross, off, two, units, units_sent, main, two_a, two_b, over = call(
+    coup, own, kept, cross, off, two, units, units_sent, main, two_a, two_b, over, two_over = call(
         pack_rest,
         "pack_rest",
         shapes,
@@ -1005,17 +1007,8 @@
     most = jnp.max(jnp.sum(needed(fill_one, live_one).reshape(-1, N_COUP), axis=1))
     most_two = jnp.max(jnp.sum(needed(fill_two, live_two).reshape(-1, N_TWO), axis=1))
 
-    def send_over(array):
-        got = swap(array, "lo")
-        return got, swap(got, "hi")
-
-    over_got, over_both = lax.cond(
-        (most > N_MAIN) | (most_two > N_TWO_A + N_TWO_B),
-        send_over,
-        lambda array: (array, array),
-        over,
-    )
-    main = after(main, part_of(got_first), two_hi, units_hi, tab_one, tab_two, over_got, over_both)
+    limits = jnp.stack([most, most_two])
+    main = after(main, part_of(got_first), two_hi, units_hi, tab_one, tab_two, limits)
     got_main = swap(main, "lo")
 
     half_rows = HALF_U * TILE
@@ -1042,7 +1035,18 @@
     part = call(third_kernel, "second_front_part", tiles(G_NONE), [SMEM] + [VMEM] * 4, VMEM, [block])(
         tab_two, s_own, units, units_hi, rows_second
     )
-    own_sent = after(own_sent, part_of(got_main), part)
+
+    def send_two(array):
+        got = swap(array, "lo")
+        return got, swap(got, "hi")
+
+    over_got = lax.cond(
+        limits[0] > N_MAIN, lambda array: swap(array, "lo"), lambda array: array, after(over, part)
+    )
+    two_over, two_over_both = lax.cond(
+        limits[1] > N_TWO_A + N_TWO_B, send_two, lambda array: (array, array), after(two_over, part)
+    )
+    own_sent = after(own_sent, part_of(got_main), over_got, two_over, two_over_both)
     got_own = swap(own_sent, "lo")
 
 
@@ -1100,7 +1104,7 @@
     two_b_both = swap(got_two_b, "hi")
     rows_wide = pltpu.VMEM((WIDE, SECOND), F32)
     halves = [pltpu.VMEM((SECOND, SECOND), jnp.bfloat16)] * 2
-    sent_two = [pltpu.VMEM((n, TILE, TILE), F32) for n in (N_TWO_A, N_TWO_B, N_OVER)]
+    sent_two = [pltpu.VMEM((n, TILE, TILE), F32) for n in (N_TWO_A, N_TWO_B, N_TWO_OVER)]
     whole_two = pltpu.VMEM((N_TWO, TILE, TILE), F32)
     panel_two, schur, rest = call(
         rows_kernel,
@@ -1119,7 +1123,7 @@
             pltpu.VMEM((3, WIDE, SECOND), F32),
             pltpu.SemaphoreType.DMA((9,)),
         ],
-    )(tab_two, part, s_oth_far, inv_high, inv_low, two, got_two_a, got_two_b, over_got, two_hi)
+    )(tab_two, part, s_oth_far, inv_high, inv_low, two, got_two_a, got_two_b, two_over, two_hi)
     schur_two = call(
         last_kernel,
         "second_front_last",
@@ -1136,7 +1140,7 @@
             pltpu.SemaphoreType.DMA,
         ],
         input_output_aliases={1: 0},
-    )(tab_two, schur, rest, panel_two, inv_high, inv_low, two_a_both, two_b_both, over_both)
+    )(tab_two, schur, rest, panel_two, inv_high, inv_low, two_a_both, two_b_both, two_over_both)
     return (
         lower_one[None, None],
         panel_one[None, None],

time: 376 us -> 377 us (level)
  transfers between devices with their start and end apart: 15 -> 15, of which waited for: 6 -> 6; matrix products, arithmetic and copies ran while one was open for 4% -> 5% of each run, Pallas kernels for 46% -> 46%
where the time goes in v1:
time: 377 us; the launch traced here: 371 us
  Pallas kernels  183 us (49%)
  waiting for transfers between devices  139 us (37%)
  local copies, waits for them, and re-layouts  18.3 us (5%)
  starting transfers between devices  16.7 us (4%)
  other arithmetic  11.6 us (3%)
    pallas_call x10, Pallas kernels, call(): return lambda *args: run(*args, *waits)  183 us
    ppermute x15, waiting for transfers between devices, swap(): return lax.ppermute(array, axis, [(i, i ^ size // 2) for i in range(size)])  139 us
    ppermute x15, starting transfers between devices, swap(): return lax.ppermute(array, axis, [(i, i ^ size // 2) for i in range(size)])  16.7 us
  transfers between devices with their start and end apart: 15, of which 6 were waited for; matrix products, arithmetic and copies ran while one was open for 5% of the time, Pallas kernels for 46%

profile of v1, /device:TPU:0, one launch (start us, length us, event | category | flops | bytes accessed | tf_op | source)
XLA Modules:
  0.0 371.4 jit_solution(15019529908855002972)
XLA Ops:
  0.7 0.7 fusion.23
  1.6 0.8 broadcast_add_fusion.15
  2.6 0.8 compare_select_fusion.2
  4.5 4.5 %pack_first.1.refs_6_ = f32[4744,128]{1,0:T(8,128)} custom-call(s32[9]{0:T(128)} %pad_add_fusion.refs_0_, f32[1024,1024]{1,0:T(8,128)} %bitcast.49, f32[384,768]{1,0:T(8,128)} %bitcast.54), custom_call_target="tpu_custom_call" | custom-call | flops 1 | bytes 1 | tf_op jit(solution)/shard_map/pack_first/pallas_call | solution.py:825
  9.0 4.1 %collective-permute-start.3 = (f32[4744,128]{1,0:T(8,128)}, f32[4744,128]{1,0:T(8,128)}, u32[]{:S(2)}, u32[]{:S(2)}) collective-permute-start(f32[4744,128]{1,0:T(8,128)} %pack_first.1.refs_6_), channel_id=1, source_target_pairs={{0,16},{4,20},{8,24},{12,28},{16,0},{20,4},{24,8},{28,12},{1,17},{... | collective-permute-start | bytes 7286792 | tf_op jit(solution)/shard_map/ppermute | solution.py:786
  13.8 0.7 compare_convert_fusion.1
  15.2 0.6 dynamic_slice.39
  15.8 0.6 compare_convert_fusion
  17.1 0.6 concatenate.14.refs_0_
  17.7 13.5 %pack_rest.1 = (f32[36,128,128]{2,1,0:T(8,128)}, f32[21,128,128]{2,1,0:T(8,128)}, f32[36,128,128]{2,1,0:T(8,128)}, f32[36,128,128]{2,1,0:T(8,128)}, f32[15,128,1...) custom-call(s32[84]{0:T(128)} %concatenate.14.refs_0_, ...), custom_call_target="tpu_custom_call" | custom-call | flops 1 | bytes 1 | tf_op jit(solution)/shard_map/pack_rest/pallas_call | solution.py:825
  31.2 1.6 collective-permute-start.4
  38.8 0.7 reduce_max.19
  39.5 0.7 reduce_max.18
  40.1 1.3 concatenate.13.refs_0_.refs_4_
  41.4 1.3 concatenate.16.refs_0_.refs_5_
  42.7 1.9 pad_add_fusion.1.refs_6_
  44.6 73.6 %collective-permute-done.3.refs_2_ = f32[4744,128]{1,0:T(8,128)} collective-permute-done((f32[4744,128]{1,0:T(8,128)}, f32[4744,128]{1,0:T(8,128)}, u32[]{:S(2)}, u32[]{:S(2)}) %collective-permute-start.3) | collective-permute-done | bytes 2428960 | tf_op jit(solution)/shard_map/ppermute | solution.py:786
  118.2 1.3 slice.24.refs_1_
  119.5 0.7 copy-done.8
  120.6 57.1 %first_front_own.1 = (f32[384,768]{1,0:T(8,128)}, bf16[768,768]{1,0:T(8,128)(2,1)}, bf16[768,768]{1,0:T(8,128)(2,1)}, bf16[768,768]{1,0:T(8,128)(2,1)}, bf16[768...) custom-call(s32[250]{0:T(256)} %concatenate.13.refs_0_.refs_4_, ...), custom_call_target="tpu_custom_call" | custom-call | flops 1 | bytes 1 | tf_op jit(solution)/shard_map/first_front_own/pallas_call | solution.py:825
  177.7 1.6 collective-permute-start.5
  180.6 12.3 %second_front_part.1.refs_1_ = f32[144,128,128]{2,1,0:T(8,128)} custom-call(s32[689]{0:T(1024)} %concatenate.16.refs_0_.refs_5_, f32[2312,128]{1,0:T(8,128)} %get-tuple-element.49.refs_1_, f32[704,128]{1,0:T(8,128)} %get-tuple-element.50.refs_2_, f32[704,128]{1,0:T(8,128)} %copy-done.8, f32[384,2304]{1,0:T(8,128)} %bitcast.52), custom_call_target="tpu_custom_call" | custom-call | flops 1 | bytes 1 | tf_op jit(solution)/shard_map/second_front_part/pallas_call | solution.py:825
  192.9 1.6 conditional.3
  192.9 1.6 copy.62
  194.5 13.4 %collective-permute-done.7.refs_2_ = f32[30,128,128]{2,1,0:T(8,128)S(1)} collective-permute-done((f32[30,128,128]{2,1,0:T(8,128)}, f32[30,128,128]{2,1,0:T(8,128)S(1)}, u32[]{:S(2)}, u32[]{:S(2)}) %collective-permute-start.7) | collective-permute-done | bytes 1966112 | tf_op jit(solution)/shard_map/ppermute | solution.py:786
  207.8 0.6 slice_bitcast_fusion.refs_1_
  208.5 0.6 copy-done.1
  209.1 1.0 copy-done.2
  210.1 9.7 %first_front_other.2.refs_8_.refs_3_ = f32[18,128,128]{2,1,0:T(8,128)} custom-call(s32[250]{0:T(256)} %concatenate.13.refs_0_.refs_4_, f32[72,128,128]{2,1,0:T(8,128)} %get-tuple-element.51.refs_1_, f32[30,128,128]{2,1,0:T(8,128)} %copy-done.1, f32[6,128,128]{2,1,0:T(8,128)S(1)} %get-tuple-element.164.refs_2_.refs_3_, ...), custom_call_target="tpu_custom_call" | custom-call | flops 1 | bytes 1 | tf_op jit(solution)/shard_map/first_front_other/pallas_call | solution.py:825
  219.8 1.3 collective-permute-start.8
  221.1 9.7 %first_front_other.3.refs_4_ = f32[18,128,128]{2,1,0:T(8,128)} custom-call(s32[250]{0:T(256)} %concatenate.13.refs_0_.refs_4_, f32[72,128,128]{2,1,0:T(8,128)} %get-tuple-element.51.refs_1_, f32[30,128,128]{2,1,0:T(8,128)} %copy-done.1, f32[6,128,128]{2,1,0:T(8,128)S(1)} %get-tuple-element.164.refs_2_.refs_3_, bf16[768,768]{1,0:T(8,128)(2,1)} %get-tuple-element.55.refs_4_, ...), custom_call_target="tpu_custom_call" | custom-call | flops 1 | bytes 1 | tf_op jit(solution)/shard_map/first_front_other/pallas_call | solution.py:825
  230.8 0.8 collective-permute-start.9
  231.7 30.3 %collective-permute-done.10.refs_1_.refs_7_ = f32[2312,128]{1,0:T(8,128)} collective-permute-done((f32[2312,128]{1,0:T(8,128)}, f32[2312,128]{1,0:T(8,128)}, u32[]{:S(2)}, u32[]{:S(2)}) %collective-permute-start.10) | collective-permute-done | bytes 1183776 | tf_op jit(solution)/shard_map/ppermute | solution.py:786
  262.0 0.9 collective-permute-start.12
  263.0 17.5 %collective-permute-done.11.refs_8_.refs_1_ = f32[704,128]{1,0:T(8,128)} collective-permute-done((f32[704,128]{1,0:T(8,128)}, f32[704,128]{1,0:T(8,128)}, u32[]{:S(2)}, u32[]{:S(2)}) %collective-permute-start.11) | collective-permute-done | bytes 360480 | tf_op jit(solution)/shard_map/ppermute | solution.py:786
  280.5 1.1 collective-permute-start.13
  281.6 1.0 copy-done.3
  283.0 17.2 %second_front_more.1.refs_4_.refs_1_ = f32[144,128,128]{2,1,0:T(8,128)} custom-call(s32[689]{0:T(1024)} %concatenate.16.refs_0_.refs_5_, f32[144,128,128]{2,1,0:T(8,128)} %second_front_part.1.refs_1_, f32[2312,128]{1,0:T(8,128)} %copy-done.2, f32[18,128,128]{2,1,0:T(8,128)} %first_front_other.2.refs_8_.refs_3_, f32[18,128,128]{2,1,0:T(8,128)} %first_front_other.3.refs_4_, ...), custom_call_target="tpu_custom_call" | custom-call | flops 1 | bytes 1 | tf_op jit(solution)/shard_map/second_front_more/pallas_call | solution.py:825
  300.3 4.5 %collective-permute-done.13.refs_2_.refs_3_ = f32[704,128]{1,0:T(8,128)} collective-permute-done((f32[704,128]{1,0:T(8,128)}, f32[704,128]{1,0:T(8,128)}, u32[]{:S(2)}, u32[]{:S(2)}) %collective-permute-start.13) | collective-permute-done | bytes 360480 | tf_op jit(solution)/shard_map/ppermute | solution.py:786
  304.8 1.0 copy-done
  305.9 2.6 collective-permute-start.15
  308.5 0.9 collective-permute-start.16
  309.5 36.9 %second_front_pivot.1 = (f32[192,768]{1,0:T(8,128)}, bf16[768,768]{1,0:T(8,128)(2,1)}, bf16[768,768]{1,0:T(8,128)(2,1)}) custom-call(s32[689]{0:T(1024)} %concatenate.16.refs_0_.refs_5_, f32[144,128,128]{2,1,0:T(8,128)} %second_front_more.1.refs_4_.refs_1_, f32[2312,128]{1,0:T(8,128)} %copy-done, f32[704,128]{1,0:T(8,128)} %collective-permute-done.13.refs_2_.refs_3_, ...), custom_call_target="tpu_custom_call" | custom-call | flops 1 | bytes 1 | tf_op jit(solution)/shard_map/second_front_pivot/pallas_call | solution.py:825
  346.5 0.7 copy-done.9
  347.4 1.1 collective-permute-start.17
  348.6 13.8 %second_front_rows.1 = (f32[384,768]{1,0:T(8,128)}, f32[384,1536]{1,0:T(8,128)}, f32[384,768]{1,0:T(8,128)}) custom-call(s32[689]{0:T(1024)} %concatenate.16.refs_0_.refs_5_, f32[144,128,128]{2,1,0:T(8,128)} %second_front_more.1.refs_4_.refs_1_, f32[2312,128]{1,0:T(8,128)} %copy-done, bf16[768,768]{1,0:T(8,128)(2,1)} %get-tuple-element.67.refs_3_.refs_4_, ...), custom_call_target="tpu_custom_call" | custom-call | flops 1 | bytes 1 | tf_op jit(solution)/shard_map/second_front_rows/pallas_call | solution.py:825
  362.3 0.8 copy-done.11
  363.2 7.9 %second_front_last.1 = f32[384,1536]{1,0:T(8,128)} custom-call(s32[689]{0:T(1024)} %concatenate.16.refs_0_.refs_5_, f32[384,1536]{1,0:T(8,128)} %get-tuple-element.70.refs_1_, f32[384,768]{1,0:T(8,128)} %get-tuple-element.71.refs_2_, f32[384,768]{1,0:T(8,128)} %get-tuple-element.69.refs_3_, ...), custom_call_target="tpu_custom_call", output_to_operand_aliasing={{}: (1, {})} | custom-call | flops 1 | bytes 1 | tf_op jit(solution)/shard_map/second_front_last/pallas_call | solution.py:825
  (145 shorter events, 10.5 us)
Async XLA Ops:
  4.5 8.6 %copy-start.14 = (s32[4,4]{1,0:T(4,128)S(1)}, s32[4,4]{1,0:T(4,128)}, u32[]{:S(2)}) copy-start(s32[4,4]{1,0:T(4,128)} %param.24) | copy-start | bytes 196
  4.5 9.3 %copy-start.12 = (s32[4,4,12,6]{2,1,3,0:T(4,128)S(1)}, s32[4,4,12,6]{2,1,3,0:T(4,128)}, u32[]{:S(2)}) copy-start(s32[4,4,12,6]{2,1,3,0:T(4,128)} %param.22) | copy-start | bytes 13828
  4.5 9.3 %copy-start.13 = (s32[2,4,12,6]{2,1,3,0:T(4,128)S(1)}, s32[2,4,12,6]{2,1,3,0:T(4,128)}, u32[]{:S(2)}) copy-start(s32[2,4,12,6]{2,1,3,0:T(4,128)} %param.23) | copy-start | bytes 6916
  4.5 10.7 %copy-start.15 = (s32[2,4]{1,0:T(2,128)S(1)}, s32[2,4]{1,0:T(2,128)}, u32[]{:S(2)}) copy-start(s32[2,4]{1,0:T(2,128)} %param.25) | copy-start | bytes 100
  9.0 109.2 %collective-permute-start.3 = (f32[4744,128]{1,0:T(8,128)}, f32[4744,128]{1,0:T(8,128)}, u32[]{:S(2)}, u32[]{:S(2)}) collective-permute-start(f32[4744,128]{1,0:T(8,128)} %pack_first.1.refs_6_), channel_id=1, source_target_pairs={{0,16},{4,20},{8,24},{12,28},{16,0},{20,4},{24,8},{28,12},{1,17},{... | collective-permute-start | bytes 7286792 | tf_op jit(solution)/shard_map/ppermute | solution.py:786
  31.2 88.3 %collective-permute-start.4 = (f32[704,128]{1,0:T(8,128)}, f32[704,128]{1,0:T(8,128)S(1)}, u32[]{:S(2)}, u32[]{:S(2)}) collective-permute-start(f32[704,128]{1,0:T(8,128)} %get-tuple-element.50.refs_2_), channel_id=1, source_target_pairs={{0,2},{1,3},{2,0},{3,1},{4,6},{5,7},{6,4},{7,5},{8,10},{9,11},{10,... | collective-permute-start | bytes 1081352 | tf_op jit(solution)/shard_map/ppermute | solution.py:786
  32.8 86.7 %collective-permute-start.6 = (f32[18,128,128]{2,1,0:T(8,128)}, f32[18,128,128]{2,1,0:T(8,128)S(1)}, u32[]{:S(2)}, u32[]{:S(2)}) collective-permute-start(f32[18,128,128]{2,1,0:T(8,128)} %get-tuple-element.53.refs_5_), channel_id=1, source_target_pairs={{0,2},{1,3},{2,0},{3,1},{4,6},{5,7},{6,4},{7,5},{8,10},{9,11},{10,... | collective-permute-start | bytes 3538952 | tf_op jit(solution)/shard_map/ppermute | solution.py:786
  119.4 0.7 copy-start.8
  119.5 1.1 copy-start.5
  120.6 87.2 %collective-permute-start.7 = (f32[30,128,128]{2,1,0:T(8,128)}, f32[30,128,128]{2,1,0:T(8,128)S(1)}, u32[]{:S(2)}, u32[]{:S(2)}) collective-permute-start(f32[30,128,128]{2,1,0:T(8,128)} %after.8), channel_id=1, source_target_pairs={{0,16},{4,20},{8,24},{12,28},{16,0},{20,4},{24,8},{28,12},{1,17},{... | collective-permute-start | bytes 5898248 | tf_op jit(solution)/shard_map/ppermute | solution.py:786
  177.7 31.4 %collective-permute-start.5 = (f32[2312,128]{1,0:T(8,128)}, f32[2312,128]{1,0:T(8,128)S(1)}, u32[]{:S(2)}, u32[]{:S(2)}) collective-permute-start(f32[2312,128]{1,0:T(8,128)} %get-tuple-element.49.refs_1_), channel_id=1, source_target_pairs={{0,2},{1,3},{2,0},{3,1},{4,6},{5,7},{6,4},{7,5},{8,10},{9,11},{10,... | collective-permute-start | bytes 3551240 | tf_op jit(solution)/shard_map/ppermute | solution.py:786
  207.8 1.3 copy-start.1
  209.1 52.9 %collective-permute-start.10 = (f32[2312,128]{1,0:T(8,128)}, f32[2312,128]{1,0:T(8,128)}, u32[]{:S(2)}, u32[]{:S(2)}) collective-permute-start(f32[2312,128]{1,0:T(8,128)} %after.11.refs_9_), channel_id=1, source_target_pairs={{0,16},{4,20},{8,24},{12,28},{16,0},{20,4},{24,8},{28,12},{1,17},{... | collective-permute-start | bytes 3551240 | tf_op jit(solution)/shard_map/ppermute | solution.py:786
  209.1 1.0 copy-start.2
  219.8 61.8 %collective-permute-start.8 = (f32[18,128,128]{2,1,0:T(8,128)}, f32[18,128,128]{2,1,0:T(8,128)S(1)}, u32[]{:S(2)}, u32[]{:S(2)}) collective-permute-start(f32[18,128,128]{2,1,0:T(8,128)} %first_front_other.2.refs_8_.refs_3_), channel_id=1, source_target_pairs={{0,2},{1,3},{2,0},{3,1},{4,6},{5,7},{6,4},{7,5},{8,10},{9,11},{10,... | collective-permute-start | bytes 3538952 | tf_op jit(solution)/shard_map/ppermute | solution.py:786
  230.8 50.8 %collective-permute-start.9 = (f32[18,128,128]{2,1,0:T(8,128)}, f32[18,128,128]{2,1,0:T(8,128)S(1)}, u32[]{:S(2)}, u32[]{:S(2)}) collective-permute-start(f32[18,128,128]{2,1,0:T(8,128)} %first_front_other.3.refs_4_), channel_id=1, source_target_pairs={{0,2},{1,3},{2,0},{3,1},{4,6},{5,7},{6,4},{7,5},{8,10},{9,11},{10,... | collective-permute-start | bytes 3538952 | tf_op jit(solution)/shard_map/ppermute | solution.py:786
  262.0 42.8 %collective-permute-start.12 = (f32[2312,128]{1,0:T(8,128)}, f32[2312,128]{1,0:T(8,128)S(1)}, u32[]{:S(2)}, u32[]{:S(2)}) collective-permute-start(f32[2312,128]{1,0:T(8,128)} %collective-permute-done.10.refs_1_.refs_7_), channel_id=1, source_target_pairs={{0,2},{1,3},{2,0},{3,1},{4,6},{5,7},{6,4},{7,5},{8,10},{9,11},{10,... | collective-permute-start | bytes 3551240 | tf_op jit(solution)/shard_map/ppermute | solution.py:786
  263.0 17.5 %collective-permute-start.11 = (f32[704,128]{1,0:T(8,128)}, f32[704,128]{1,0:T(8,128)}, u32[]{:S(2)}, u32[]{:S(2)}) collective-permute-start(f32[704,128]{1,0:T(8,128)} %after.12), channel_id=1, source_target_pairs={{0,16},{4,20},{8,24},{12,28},{16,0},{20,4},{24,8},{28,12},{1,17},{... | collective-permute-start | bytes 1081352 | tf_op jit(solution)/shard_map/ppermute | solution.py:786
  280.5 24.3 %collective-permute-start.13 = (f32[704,128]{1,0:T(8,128)}, f32[704,128]{1,0:T(8,128)}, u32[]{:S(2)}, u32[]{:S(2)}) collective-permute-start(f32[704,128]{1,0:T(8,128)} %collective-permute-done.11.refs_8_.refs_1_), channel_id=1, source_target_pairs={{0,2},{1,3},{2,0},{3,1},{4,6},{5,7},{6,4},{7,5},{8,10},{9,11},{10,... | collective-permute-start | bytes 1081352 | tf_op jit(solution)/shard_map/ppermute | solution.py:786
  281.6 1.0 copy-start.3
  281.6 1.4 copy-start.4
  283.0 17.3 %collective-permute-start.14 = (f32[5,128,128]{2,1,0:T(8,128)}, f32[5,128,128]{2,1,0:T(8,128)S(1)}, u32[]{:S(2)}, u32[]{:S(2)}) collective-permute-start(f32[5,128,128]{2,1,0:T(8,128)} %after.13), channel_id=1, source_target_pairs={{0,16},{4,20},{8,24},{12,28},{16,0},{20,4},{24,8},{28,12},{1,17},{... | collective-permute-start | bytes 983048 | tf_op jit(solution)/shard_map/ppermute | solution.py:786
  300.3 4.5 %copy-start.10 = (f32[5,128,128]{2,1,0:T(8,128)}, f32[5,128,128]{2,1,0:T(8,128)S(1)}, u32[]{:S(2)}) copy-start(f32[5,128,128]{2,1,0:T(8,128)S(1)} %collective-permute-done.14.refs_1_.refs_6_) | copy-start | bytes 983044
  304.8 1.1 copy-start
  305.9 40.6 %collective-permute-start.15 = (f32[11,128,128]{2,1,0:T(8,128)}, f32[11,128,128]{2,1,0:T(8,128)S(1)}, u32[]{:S(2)}, u32[]{:S(2)}) collective-permute-start(f32[11,128,128]{2,1,0:T(8,128)} %after.14.refs_4_), channel_id=1, source_target_pairs={{0,16},{4,20},{8,24},{12,28},{16,0},{20,4},{24,8},{28,12},{1,17},{... | collective-permute-start | bytes 2162696 | tf_op jit(solution)/shard_map/ppermute | solution.py:786
  308.5 37.9 %collective-permute-start.16 = (f32[5,128,128]{2,1,0:T(8,128)}, f32[5,128,128]{2,1,0:T(8,128)S(1)}, u32[]{:S(2)}, u32[]{:S(2)}) collective-permute-start(f32[5,128,128]{2,1,0:T(8,128)} %copy-done.10), channel_id=1, source_target_pairs={{0,2},{1,3},{2,0},{3,1},{4,6},{5,7},{6,4},{7,5},{8,10},{9,11},{10,... | collective-permute-start | bytes 983048 | tf_op jit(solution)/shard_map/ppermute | solution.py:786
  346.4 2.2 copy-start.7
  346.4 0.7 copy-start.9
  346.4 1.0 copy-start.6
  347.4 14.9 %collective-permute-start.17 = (f32[11,128,128]{2,1,0:T(8,128)}, f32[11,128,128]{2,1,0:T(8,128)S(1)}, u32[]{:S(2)}, u32[]{:S(2)}) collective-permute-start(f32[11,128,128]{2,1,0:T(8,128)} %after.15.refs_7_), channel_id=1, source_target_pairs={{0,2},{1,3},{2,0},{3,1},{4,6},{5,7},{6,4},{7,5},{8,10},{9,11},{10,... | collective-permute-start | bytes 2162696 | tf_op jit(solution)/shard_map/ppermute | solution.py:786
  362.3 0.9 copy-start.11
